TPU v7x, 128 devices: a whole 4x4x4 slice. The times are simulated.
128 devices in a mesh: mp: 8 (over y, core), mem: 16 (over z, x).
Axes of the slice: x: 4, y: 4, z: 4, core: 2. Of those that a mesh axis runs over, the one named last changes fastest.
Arguments:
- tokens: bfloat16 [16, 8192], P(None, 'mem'), may hold values from -6 to 6
- attn_gain: bfloat16 [8192], P('mem'), may hold values from 0.099609375 to 1.8984375
- query_key_value_weight: bfloat16 [8192, 10240], P('mem', 'mp'), may hold values from -0.0625 to 0.0625
- paged_key_store: bfloat16 [2048, 8, 128, 128], P('mem', 'mp'), may hold values from -110 to 110
- paged_value_store: bfloat16 [2048, 8, 128, 128], P('mem', 'mp'), may hold values from -6 to 6
- lengths: int32 [4], replicated, may hold values from 1 to 65536, as said below
- block_table: int32 [4, 512], replicated, may hold values from -1 to 2047, as said below
- out_weight: bfloat16 [8192, 8192], P('mp', 'mem'), may hold values from -0.47851562 to 0.47851562
- mlp_gain: bfloat16 [8192], P('mem'), may hold values from 0.099609375 to 1.8984375
- gate_weight: bfloat16 [8192, 28672], P('mem', 'mp'), may hold values from -0.0625 to 0.0625
- up_weight: bfloat16 [8192, 28672], P('mem', 'mp'), may hold values from -0.0625 to 0.0625
- down_weight: bfloat16 [28672, 8192], P('mp', 'mem'), may hold values from -0.03125 to 0.03125
Outputs:
- layer_out: bfloat16 [16, 8192], P(None, 'mem')
Inputs may be any that keep to these rules, and one draw needn't show every extreme that they name: `lengths`: at least one request has exactly 65536 cached tokens. `block_table`: entry b of request r is a pool block for b < ceil(lengths[r] / 128) and -1 otherwise; no pool block is named twice in the table.
All inputs are finite; a program needn't handle non-finite values.
Results may differ from a plain program's by a relative error of at most 0.015.
The roundings to bfloat16 on the way count: a program that leaves them out, or rounds other values in their place, can miss the bound.
Values may be sent and summed in bfloat16 or wider, within the bound.
A program may use at most 64 MiB of HBM per device.

v0:
```python
import math

import jax
import jax.numpy as jnp
from jax import lax
from jax.sharding import PartitionSpec as P

EPSILON = 1e-05
ROPE_BASE = 500000.0
FLOOR_SCORE = -1e30


def rotate(values, position):
    half_dim = values.shape[-1] // 2
    inverse = jnp.exp(
        jnp.arange(half_dim, dtype=jnp.float32) * (-2.0 * math.log(ROPE_BASE) / values.shape[-1])
    )
    angle = position[..., None] * inverse
    cosine = jnp.cos(angle)
    sine = jnp.sin(angle)
    first = values[..., :half_dim]
    second = values[..., half_dim:]
    return jnp.concatenate(
        [first * cosine - second * sine, second * cosine + first * sine], axis=-1
    )


def local(
    tokens,
    attn_gain,
    query_key_value_weight,
    paged_key_store,
    paged_value_store,
    lengths,
    block_table,
    out_weight,
    mlp_gain,
    gate_weight,
    up_weight,
    down_weight,
):
    highest = lax.Precision.HIGHEST
    rows, width_part = tokens.shape
    model_width = width_part * lax.axis_size("mem")
    requests = lengths.shape[0]
    new_count = rows // requests
    slots, heads_kv, block_len, head_dim = paged_key_store.shape
    query_group = out_weight.shape[0] // (heads_kv * head_dim)
    token_f = tokens.astype(jnp.float32)
    scaled_in = (token_f * attn_gain.astype(jnp.float32)).astype(jnp.bfloat16)
    partial_proj = jnp.dot(scaled_in, query_key_value_weight, preferred_element_type=jnp.float32)
    projected_rows, square_sum = lax.psum((partial_proj, jnp.sum(token_f * token_f, axis=1)), "mem")
    inverse_one = 1.0 / jnp.sqrt(square_sum / model_width + EPSILON)
    projected_rows = (projected_rows * inverse_one[:, None]).reshape(
        requests, new_count, heads_kv, query_group + 2, head_dim
    )
    position = (lengths[:, None] + jnp.arange(new_count, dtype=jnp.int32)[None, :]).astype(
        jnp.float32
    )
    queries = rotate(projected_rows[:, :, :, :query_group], position[:, :, None, None]).astype(
        jnp.bfloat16
    )
    new_keys = rotate(projected_rows[:, :, :, query_group], position[:, :, None]).astype(
        jnp.bfloat16
    )
    new_values = projected_rows[:, :, :, query_group + 1].astype(jnp.bfloat16)
    scale = 1.0 / math.sqrt(head_dim)
    first_slot = lax.axis_index("mem") * slots
    slot_ids = first_slot + jnp.arange(slots, dtype=jnp.int32)
    max_blocks = block_table.shape[1]
    block_ids = jnp.arange(max_blocks, dtype=jnp.int32)
    request_ids = jnp.arange(requests, dtype=jnp.int32)
    in_use = (block_ids[None, :] * block_len < lengths[:, None]) & (block_table >= 0)
    matches = ((block_table[:, :, None] == slot_ids[None, None, :]) & in_use[:, :, None]).astype(
        jnp.int32
    )
    holder = jnp.sum(matches * request_ids[:, None, None], axis=(0, 1))
    block_place = jnp.sum(matches * block_ids[None, :, None], axis=(0, 1))
    living = jnp.sum(matches, axis=(0, 1)) > 0
    ordering = jnp.argsort(jnp.where(living, 0, 1), stable=True)
    span = min(16, slots)
    turns = (jnp.sum(living.astype(jnp.int32)) + span - 1) // span
    state_shape = (requests, new_count, heads_kv, query_group)
    token_steps = jnp.arange(block_len, dtype=jnp.int32)

    def visit(step_index, carry):
        best, total, accum = carry
        picked = lax.dynamic_slice_in_dim(ordering, step_index * span, span)
        block_keys = paged_key_store[picked]
        block_values = paged_value_store[picked].astype(jnp.float32)
        holders = holder[picked]
        places = block_place[picked]
        alive = living[picked]
        slot_queries = queries[holders]
        scores = (
            jnp.einsum(
                "snkgd,skjd->snkgj", slot_queries, block_keys, preferred_element_type=jnp.float32
            )
            * scale
        )
        token_pos = places[:, None] * block_len + token_steps[None, :]
        usable = (alive[:, None] & (token_pos < lengths[holders][:, None]))[:, None, None, None, :]
        scores = jnp.where(usable, scores, FLOOR_SCORE)
        owners = (holders[:, None] == request_ids[None, :]) & alive[:, None]
        slot_best = jnp.max(scores, axis=-1)
        block_best = jnp.max(
            jnp.where(owners[:, :, None, None, None], slot_best[:, None], FLOOR_SCORE), axis=0
        )
        fresh = jnp.maximum(best, block_best)
        factor = jnp.exp(best - fresh)
        weights = jnp.where(usable, jnp.exp(scores - fresh[holders][..., None]), 0.0)
        owner_f = owners.astype(jnp.float32)
        total = total * factor + jnp.einsum(
            "sr,snkg->rnkg", owner_f, jnp.sum(weights, axis=-1), precision=highest
        )
        mixed = jnp.einsum("snkgj,skjd->snkgd", weights, block_values, precision=highest)
        accum = accum * factor[..., None] + jnp.einsum(
            "sr,snkgd->rnkgd", owner_f, mixed, precision=highest
        )
        return (fresh, total, accum)

    initial = (
        jnp.full(state_shape, FLOOR_SCORE, jnp.float32),
        jnp.zeros(state_shape, jnp.float32),
        jnp.zeros(state_shape + (head_dim,), jnp.float32),
    )
    best, total, accum = lax.fori_loop(0, turns, visit, initial)
    overall = lax.pmax(best, "mem")
    shrink = jnp.exp(best - overall)
    total, accum = lax.psum((total * shrink, accum * shrink[..., None]), "mem")
    best = overall
    causal = jnp.arange(new_count)[None, :] <= jnp.arange(new_count)[:, None]
    own_scores = (
        jnp.einsum("rnkgd,rmkd->rnkgm", queries, new_keys, preferred_element_type=jnp.float32)
        * scale
    )
    causal_mask = causal[None, :, None, None, :]
    own_scores = jnp.where(causal_mask, own_scores, FLOOR_SCORE)
    joined = jnp.maximum(best, jnp.max(own_scores, axis=-1))
    own_weights = jnp.where(causal_mask, jnp.exp(own_scores - joined[..., None]), 0.0)
    factor = jnp.exp(best - joined)
    total = total * factor + jnp.sum(own_weights, axis=-1)
    accum = accum * factor[..., None] + jnp.einsum(
        "rnkgm,rmkd->rnkgd", own_weights, new_values.astype(jnp.float32), precision=highest
    )
    attended = (
        (accum / total[..., None])
        .astype(jnp.bfloat16)
        .reshape(rows, heads_kv * query_group * head_dim)
    )
    combined = lax.psum(jnp.dot(attended, out_weight, preferred_element_type=jnp.float32), "mp")
    after_attn = (token_f + combined).astype(jnp.bfloat16)
    after_f = after_attn.astype(jnp.float32)
    scaled_mid = (after_f * mlp_gain.astype(jnp.float32)).astype(jnp.bfloat16)
    gate_local = jnp.dot(scaled_mid, gate_weight, preferred_element_type=jnp.float32)
    up_local = jnp.dot(scaled_mid, up_weight, preferred_element_type=jnp.float32)
    square_mid = jnp.sum(after_f * after_f, axis=1)
    gate_whole, up_whole, square_whole = lax.psum((gate_local, up_local, square_mid), "mem")
    inverse_two = 1.0 / jnp.sqrt(square_whole / model_width + EPSILON)
    hidden = (
        jax.nn.silu(gate_whole * inverse_two[:, None]) * (up_whole * inverse_two[:, None])
    ).astype(jnp.bfloat16)
    down_total = lax.psum(jnp.dot(hidden, down_weight, preferred_element_type=jnp.float32), "mp")
    return (after_f + down_total).astype(jnp.bfloat16)


def solution(mesh):
    return jax.shard_map(
        local,
        mesh=mesh,
        in_specs=(
            P(None, "mem"),
            P("mem"),
            P("mem", "mp"),
            P("mem", "mp", None, None),
            P("mem", "mp", None, None),
            P(),
            P(),
            P("mp", "mem"),
            P("mem"),
            P("mem", "mp"),
            P("mem", "mp"),
            P("mp", "mem"),
        ),
        out_specs=P(None, "mem"),
        check_vma=False,
    )
```

profile of v0, /device:TPU:1, one launch (start us, length us, event | category | flops | bytes accessed | tf_op | source)
XLA Modules:
  0.0 444.7 jit_solution(787136088362462810)
XLA Ops:
  6.5 0.8 convert_element_type.74
  7.9 1.6 fusion.48
  9.6 0.8 compare_and_fusion.1
  10.4 1.4 select_reduce_fusion.1
  13.1 0.8 fusion.35
  13.9 0.7 add_convert_fusion.1
  14.7 35.3 %psum.64 = f32[16]{0:T(128)S(1)} all-reduce(f32[16]{0:T(128)S(1)} %fusion.35), channel_id=1, replica_groups=mesh['mp'=8,'mem'=16] {'mem'}, use_global_device_ids=true, to_apply=%region_7.8 | all-reduce | flops 16 | bytes 128 | tf_op jit(solution)/shard_map/psum | solution.py:52
  50.6 2.6 sort.17
  53.4 40.3 %all-reduce.5.cloned.1.call-done = f32[16,1280]{1,0:T(8,128)} async-done(((f32[16,1280]{1,0:T(8,128)}), f32[16,1280]{1,0:T(8,128)}) %all-reduce.5.cloned.1.call-update) | async-done | bytes 81936 | tf_op jit(solution)/shard_map/psum | solution.py:52
  93.7 1.0 broadcast_multiply_fusion.1
  94.9 37.9 %while.15 = (s32[]{:T(128)}, f32[4,4,1,8]{3,1,0,2:T(4,128)S(1)}, f32[4,4,1,8]{3,1,0,2:T(4,128)S(1)}, f32[4,4,1,8,128]{4,0,3,1,2:T(4,128)S(1)}, s32[]{:T(128)}, /...) while((s32[]{:T(128)}, f32[4,4,1,8]{3,1,0,2:T(4,128)S(1)}, ...), condition=%wide.region_12.13_spmd.clone, body=%wide.region_8.12_spmd.clone.sunk | while | flops 121179888 | bytes 5027927 | solution.py:127
  96.3 2.8 gather_fusion.2
  99.1 1.3 gather_fusion.3
  103.6 2.8 gather_fusion.7
  108.9 2.8 gather_fusion.2
  111.8 1.3 gather_fusion.3
  116.3 2.8 gather_fusion.7
  121.6 2.8 gather_fusion.2
  124.4 1.3 gather_fusion.3
  128.9 2.8 gather_fusion.7
  132.8 79.9 %pmax.7 = f32[4,4,1,8]{3,1,0,2:T(4,128)S(1)} all-reduce(f32[4,4,1,8]{3,1,0,2:T(4,128)S(1)} %get-tuple-element.88), channel_id=1, replica_groups=mesh['mp'=8,'mem'=16] {'mem'}, use_global_device_ids=true, to_apply=%region_13.14 | all-reduce | flops 128 | bytes 1024 | tf_op jit(solution)/shard_map/pmax | solution.py:128
  214.1 29.0 %psum.66 = f32[4,4,1,8]{3,1,0,2:T(4,128)S(1)} all-reduce(f32[4,4,1,8]{3,1,0,2:T(4,128)S(1)} %get-tuple-element.226), channel_id=1, replica_groups=mesh['mp'=8,'mem'=16] {'mem'}, use_global_device_ids=true, to_apply=%region_16.17 | all-reduce | flops 128 | bytes 1024 | tf_op jit(solution)/shard_map/psum | solution.py:130
  243.2 55.3 %all-reduce.7.cloned.1.call-done = f32[4,4,1,8,128]{4,3,1,0,2:T(8,128)} async-done(((f32[4,4,1,8,128]{4,3,1,0,2:T(8,128)}), f32[4,4,1,8,128]{4,3,1,0,2:T(8,128)}) %all-reduce.7.cloned.1.call-update) | async-done | bytes 65552 | tf_op jit(solution)/shard_map/psum | solution.py:130
  298.6 1.2 fusion.28
  299.8 1.5 fusion.40
  301.2 22.7 %psum.67 = f32[16,512]{1,0:T(8,128)S(1)} all-reduce(f32[16,512]{1,0:T(8,128)S(1)} %fusion.40), channel_id=1, replica_groups=mesh['mp'=8,'mem'=16] {'mp'}, use_global_device_ids=true, to_apply=%region_18.19 | all-reduce | flops 8192 | bytes 65536 | tf_op jit(solution)/shard_map/psum | solution.py:151
  324.1 3.5 fusion.54
  327.6 1.3 fusion.56
  328.9 31.1 %psum.69 = f32[16]{0:T(128)S(1)} all-reduce(f32[16]{0:T(128)S(1)} %get-tuple-element.218), channel_id=1, replica_groups=mesh['mp'=8,'mem'=16] {'mem'}, use_global_device_ids=true, to_apply=%region_21.22 | all-reduce | flops 16 | bytes 128 | tf_op jit(solution)/shard_map/psum | solution.py:158
  360.0 51.9 %all-reduce.9.cloned.1.call-done = (f32[16,3584]{1,0:T(8,128)}, f32[16,3584]{1,0:T(8,128)}) async-done(((f32[16,3584]{1,0:T(8,128)}, f32[16,3584]{1,0:T(8,128)}), (f32[16,3584]{1,0:T(8,128)}, f32[16,3584]{1,0:T(8,128)})) %all-reduce.9.cloned.1.call-update) | async-done | bytes 458768 | tf_op jit(solution)/shard_map/psum | solution.py:158
  411.9 2.9 fusion.31
  414.8 22.7 %psum.71 = f32[16,512]{1,0:T(8,128)S(1)} all-reduce(f32[16,512]{1,0:T(8,128)S(1)} %fusion.31), channel_id=1, replica_groups=mesh['mp'=8,'mem'=16] {'mp'}, use_global_device_ids=true, to_apply=%region_23.24 | all-reduce | flops 8192 | bytes 65536 | tf_op jit(solution)/shard_map/psum | solution.py:163
  (108 shorter events, 21.2 us)
Async XLA Ops:
  6.5 1.3 copy-start
  6.5 87.1 %all-reduce.5.cloned.1.call-start = ((), (), s32[]{:S(2)}) async-start(), calls=%async_computation | async-start | bytes 163840 | tf_op jit(solution)/shard_map/psum | solution.py:52
  9.5 289.1 %all-reduce.7.cloned.1.call-start = ((), (), s32[]{:S(2)}) async-start(), calls=%async_computation.1 | async-start | bytes 131072 | tf_op jit(solution)/shard_map/psum | solution.py:130
  94.9 229.1 %copy-start.2 = (bf16[16,512]{1,0:T(8,128)(2,1)S(1)}, bf16[16,512]{1,0:T(8,128)(2,1)}, u32[]{:S(2)}) copy-start(bf16[16,512]{1,0:T(8,128)(2,1)} %param.14) | copy-start | bytes 49156
  214.0 197.8 %all-reduce.9.cloned.1.call-start = ((), (), s32[]{:S(2)}) async-start(), calls=%async_computation.2 | async-start | bytes 917504 | tf_op jit(solution)/shard_map/psum | solution.py:158
  324.0 3.6 copy-start.1
Sparse Core Ops, SparseCore 0:
  10.6 83.0 all-reduce.4
  214.1 84.4 all-reduce.6
  329.0 82.8 all-reduce.8
where the time goes:
time: 448 us; the launch traced here: 445 us
  blocking collectives  221 us (49%)
  waiting for transfers between devices  148 us (33%)
  local copies, waits for them, and re-layouts  31.6 us (7%)
  matrix products  17.1 us (4%)
  between operations  13.9 us (3%)
  other arithmetic  13.3 us (3%)
    pmax x1, blocking collectives, local(): overall = lax.pmax(best, 'mem')  79.9 us
    psum x1, waiting for transfers between devices, local(): total, accum = lax.psum((total * shrink, accum * shrink[..., None]), 'mem')  55.3 us
    psum x1, waiting for transfers between devices, local(): lax.psum((gate_local, up_local, square_mid), 'mem')  51.9 us
    psum x1, waiting for transfers between devices, local(): lax.psum((partial_proj, jnp.sum(token_f * token_f, axis=1)), 'mem')  40.3 us
    psum x1, blocking collectives, local(): lax.psum((partial_proj, jnp.sum(token_f * token_f, axis=1)), 'mem')  35.3 us
    psum x1, blocking collectives, local(): lax.psum((gate_local, up_local, square_mid), 'mem')  31.1 us
    psum x1, blocking collectives, local(): total, accum = lax.psum((total * shrink, accum * shrink[..., None]), 'mem')  29 us
    psum x1, blocking collectives, local(): lax.psum(jnp.dot(attended, out_weight, preferred_element_type=jnp.float32...  22.7 us
  transfers between devices with their start and end apart: 3, of which 3 were waited for; matrix products, arithmetic and copies ran while one was open for 2% of the time, Pallas kernels for 0%

commit v1 on v0

v1 whole, which is shorter than its diff:
```python
import functools
import math

import jax
import jax.numpy as jnp
import numpy as np
from jax import lax
from jax.experimental import pallas as pl
from jax.experimental.pallas import tpu as pltpu
from jax.sharding import PartitionSpec as P

MESH = pl.DeviceIdType.MESH
F32 = jnp.float32
BF16 = jnp.bfloat16

EPSILON = 1e-05
ROPE_BASE = 500000.0
FLOOR_SCORE = -1e30
LANES = 128
HEADS = 8
NEW = 4
REQUESTS = 4
GROUP = NEW * HEADS
OWNER = 256
TILE = 16
PIECES = 4

HALF_PI = (1.5703125, 0.000484466552734375, -6.397578377557687e-07)


def sine_cosine(angle):
    turns = jnp.floor(angle * (2.0 / math.pi) + 0.5)
    r = ((angle - turns * HALF_PI[0]) - turns * HALF_PI[1]) - turns * HALF_PI[2]
    z = r * r
    sine = r + r * z * (-1.6666654611e-1 + z * (8.3321608736e-3 + z * (-1.9515295891e-4)))
    cosine = 1.0 - 0.5 * z + z * z * (
        4.166664568298827e-2 + z * (-1.388731625493765e-3 + z * 2.443315711809948e-5)
    )
    quadrant = turns - 4.0 * jnp.floor(turns * 0.25)
    odd = (quadrant == 1.0) | (quadrant == 3.0)
    s, c = jnp.where(odd, cosine, sine), jnp.where(odd, sine, cosine)
    s = jnp.where(quadrant >= 2.0, -s, s)
    c = jnp.where((quadrant == 1.0) | (quadrant == 2.0), -c, c)
    return s, c


STEPS = 32000.0
FINE = 256.0


def code_of(value):
    return jnp.log(jnp.maximum(value, 1e-30)) * (FINE / math.log(2.0))


def value_of(code):
    return jnp.exp2(code * (1.0 / FINE))


def kernel(
    members,
    peers,
    model_width,
    lengths,
    tokens_hbm,
    gain_one,
    gain_two,
    freq_hbm,
    table_hbm,
    wqkv_hbm,
    keys_hbm,
    values_hbm,
    wout_hbm,
    wgate_hbm,
    wup_hbm,
    wdown_hbm,
    out_ref,
    tokens,
    freq,
    table,
    wqkv,
    keys,
    values,
    wout,
    wgate,
    wup,
    wdown,
    queries,
    codes,
    slot_codes,
    tops_ref,
    scores,
    s1,
    r1,
    s2,
    r2,
    s4,
    r4,
    s5,
    r5,
    token_lines,
    s5b,
    r5b,
    s5c,
    r5c,
    g6a,
    s6a,
    r6a,
    g6b,
    s6b,
    r6b,
    s7,
    r7,
    g7,
    s7b,
    r7b,
    s7c,
    r7c,
    code_sem,
    fetch_sem,
    send_sem,
    recv_sem,
):
    me = lax.axis_index("mem")
    mine = lax.axis_index("mp")
    rows = tokens.shape[0]
    slots = keys.shape[0]
    block_len = keys.shape[1]
    chunks = wgate.shape[1] // LANES
    half = s7.shape[0]

    barrier = pltpu.get_barrier_semaphore()
    for k in range(1, members):
        pl.semaphore_signal(
            barrier, inc=1, device_id={"mem": lax.rem(me + k, members)}, device_id_type=MESH
        )
    for k in range(1, peers):
        pl.semaphore_signal(
            barrier, inc=1, device_id={"mp": lax.rem(mine + k, peers)}, device_id_type=MESH
        )

    fetched = {}

    def fetch(name, source, target, pieces=1):
        size = target.shape[0] // pieces
        fetched[name] = []
        for p in range(pieces):
            index = sum(len(v) for v in fetched.values())
            part = pl.ds(p * size, size)
            copy = pltpu.make_async_copy(source.at[part], target.at[part], fetch_sem.at[index])
            copy.start()
            fetched[name].append(copy)

    def ready(*names):
        for name in names:
            for copy in fetched[name]:
                copy.wait()

    fetch("tokens", tokens_hbm, tokens)
    fetch("wqkv", wqkv_hbm, wqkv, PIECES)
    fetch("table", table_hbm, table)
    fetch("freq", freq_hbm, freq)

    def send_members(phase, source_of, target):
        for k in range(1, members):
            other = lax.rem(me + k, members)
            pltpu.make_async_remote_copy(
                src_ref=source_of(other),
                dst_ref=target,
                send_sem=send_sem.at[phase],
                recv_sem=recv_sem.at[phase],
                device_id={"mem": other},
                device_id_type=MESH,
            ).start()

    def send_peers(phase, source_of, target):
        for k in range(1, peers):
            other = lax.rem(mine + k, peers)
            pltpu.make_async_remote_copy(
                src_ref=source_of(other),
                dst_ref=target,
                send_sem=send_sem.at[phase],
                recv_sem=recv_sem.at[phase],
                device_id={"mp": other},
                device_id_type=MESH,
            ).start()

    cuts = tokens.shape[1] // LANES
    lines_own = rows // peers * cuts
    own_lines = pl.ds(pl.multiple_of(mine * lines_own, lines_own), lines_own)

    def spread(ref, array):
        for c in range(cuts):
            ref[pl.ds(c, rows, stride=cuts), :] = array[:, c * LANES : (c + 1) * LANES]

    def gather(ref):
        return jnp.concatenate([ref[pl.ds(c, rows, stride=cuts), :] for c in range(cuts)], axis=1)

    def sum_peers(phase, partial, residual, staged, landed, rounded, whole, between=None):
        spread(staged, partial)
        send_peers(
            phase, lambda other: staged.at[pl.ds(other * lines_own, lines_own)], landed.at[mine]
        )
        landed[mine] = staged[own_lines, :]
        if between is not None:
            between()
        wait_bytes(landed.at[pl.ds(0, peers - 1)], recv_sem.at[phase])
        total = landed[0]
        for j in range(1, peers):
            total = total + landed[j]
        share = (residual + total).astype(BF16).astype(F32)
        rounded[...] = share
        whole[own_lines, :] = share
        send_peers(phase + 1, lambda other: rounded, whole.at[own_lines])
        wait_bytes(whole.at[pl.ds(0, (peers - 1) * lines_own)], recv_sem.at[phase + 1])
        return share, gather(whole)

    def wait_bytes(window, semaphore):
        pltpu.make_async_copy(window, window, semaphore).wait()

    ready("tokens")
    token_f = tokens[...].astype(F32)
    scaled_in = (token_f * gain_one[...].astype(F32)[None, :]).astype(BF16)
    square_one = jnp.sum(token_f * token_f, axis=1, keepdims=True)
    ready("wqkv")
    fetch("keys", keys_hbm.at[:, 0], keys, PIECES)
    fetch("values", values_hbm.at[:, 0], values, PIECES)
    projected = jnp.dot(scaled_in, wqkv[...], preferred_element_type=F32)
    for c in range(HEADS + 2):
        s1[pl.ds(c, rows, stride=rows), :] = projected[:, c * LANES : (c + 1) * LANES]
    s1[pl.ds(HEADS + 2, rows, stride=rows), :] = jnp.broadcast_to(square_one, (rows, LANES))

    pl.semaphore_wait(barrier, members - 1 + peers - 1)

    used = HEADS + 3
    send_members(
        0, lambda other: s1.at[pl.ds(other * rows, used)], r1.at[me, pl.ds(0, used)]
    )
    r1[me] = s1[pl.ds(pl.multiple_of(me * rows, rows), rows), :]

    fetch("wout", wout_hbm, wout, 2)
    fetch("wgate", wgate_hbm, wgate, PIECES)
    fetch("wup", wup_hbm, wup, PIECES)
    fetch("wdown", wdown_hbm, wdown, PIECES)

    request, place = me // NEW, lax.rem(me, NEW)
    ready("freq")
    position = (lengths[request] + place).astype(F32)
    sine, cosine = sine_cosine(position * freq[...])
    lane_row = lax.broadcasted_iota(jnp.int32, (1, LANES), 1)
    sine = jnp.where(lane_row < LANES // 2, -sine, sine)

    ready("table")
    first_slot = me * slots
    max_blocks = table.shape[1]
    block_start = lax.broadcasted_iota(jnp.int32, (1, max_blocks), 1) * block_len
    slot_ids = first_slot + lax.broadcasted_iota(jnp.int32, (slots, max_blocks), 0)
    code = jnp.zeros((slots, max_blocks), jnp.int32)
    for r in range(REQUESTS):
        held = jnp.clip(lengths[r] - block_start, 0, block_len)
        held = jnp.where(held > 0, held + r * OWNER, 0)
        code = code + jnp.where(table[r : r + 1, :] == slot_ids, held, 0)
    code = jnp.sum(code, axis=1, keepdims=True)
    diagonal = lax.broadcasted_iota(jnp.int32, (slots, slots), 0) == lax.broadcasted_iota(
        jnp.int32, (slots, slots), 1
    )
    code = jnp.sum(jnp.where(diagonal, code, 0), axis=0, keepdims=True)
    owner_row = code // OWNER
    codes[0:1, :] = code
    to_scalars = pltpu.make_async_copy(codes, slot_codes, code_sem)
    to_scalars.start()

    wait_bytes(r1.at[pl.ds(0, members - 1), pl.ds(0, used)], recv_sem.at[0])
    total = r1[0]
    for j in range(1, members):
        total = total + r1[j]
    inverse_one = 1.0 / jnp.sqrt(total[HEADS + 2 : HEADS + 3, :] / model_width + EPSILON)
    total = total * inverse_one
    turned = total * cosine + pltpu.roll(total, LANES // 2, 1) * sine
    head_row = lax.broadcasted_iota(jnp.int32, total.shape, 0)
    s2[...] = jnp.where(head_row <= HEADS, turned, total).astype(BF16)
    r2[me] = s2[...]
    send_members(1, lambda other: s2, r2.at[me])
    wait_bytes(r2.at[pl.ds(0, members - 1)], recv_sem.at[1])

    for r in range(REQUESTS):
        queries[r] = jnp.concatenate(
            [r2[r * NEW + t].astype(F32)[:HEADS] for t in range(NEW)], axis=0
        ).astype(BF16)
    factor = math.log2(math.e) / math.sqrt(LANES)
    lane_group = lax.broadcasted_iota(jnp.int32, (GROUP, LANES), 1)
    to_scalars.wait()
    ready("keys")

    def slot_of(slot):
        value = slot_codes[0, slot]
        return value // OWNER, lax.rem(value, OWNER)

    def score_step(step, best):
        for j in range(TILE):
            slot = step * TILE + j
            owner, count = slot_of(slot)
            score = lax.dot_general(
                queries[owner],
                keys[slot],
                (((1,), (1,)), ((), ())),
                preferred_element_type=F32,
            )
            score = jnp.where(lane_group < count, score, FLOOR_SCORE)
            scores[slot] = score
            best = jnp.where(lane_group == slot, jnp.max(score, axis=1, keepdims=True), best)
        return best

    floor = jnp.full((GROUP, LANES), FLOOR_SCORE, F32)
    slot_best = lax.fori_loop(0, slots // TILE, score_step, floor)
    best = []
    for r in range(REQUESTS):
        own = jnp.where(owner_row == r, slot_best, FLOOR_SCORE)
        best.append(jnp.broadcast_to(jnp.max(own, axis=1, keepdims=True), (GROUP, LANES)))
        tops_ref[r] = best[r]
    ready("values")

    def value_step(step, carry):
        sums, mixed = carry
        line = []
        for j in range(TILE):
            slot = step * TILE + j
            owner, _ = slot_of(slot)
            weight = jnp.exp2((scores[slot] - tops_ref[owner]) * factor)
            sums = jnp.where(lane_group == slot, jnp.sum(weight, axis=1, keepdims=True), sums)
            weight = weight.astype(BF16)
            line.append(
                jnp.concatenate(
                    [jnp.where(owner == r, weight, jnp.zeros_like(weight)) for r in range(REQUESTS)],
                    axis=0,
                )
            )
        block = values[pl.ds(step * TILE, TILE)].reshape(TILE * block_len, LANES)
        mixed = mixed + jnp.dot(
            jnp.concatenate(line, axis=1), block, preferred_element_type=F32
        )
        return sums, mixed

    slot_sums, mixed = lax.fori_loop(
        0,
        slots // TILE,
        value_step,
        (jnp.zeros((GROUP, LANES), F32), jnp.zeros((REQUESTS * GROUP, LANES), F32)),
    )
    lane_tile = lax.broadcasted_iota(jnp.int32, (HEADS, LANES), 1)
    for r in range(REQUESTS):
        own = jnp.where(owner_row == r, slot_sums, 0.0)
        whole = jnp.broadcast_to(jnp.sum(own, axis=1, keepdims=True), (GROUP, LANES))
        for t in range(NEW):
            part = slice(t * HEADS, (t + 1) * HEADS)
            i = r * NEW + t
            s4[i, :HEADS, :] = mixed[i * HEADS : (i + 1) * HEADS]
            s4[i, HEADS:, :] = jnp.where(lane_tile < LANES // 2, best[r][part], whole[part])
    send_members(2, lambda other: s4.at[other], r4.at[me])
    r4[me] = s4[me]

    row_queries = r2[me].astype(F32)[:HEADS]
    own_scores, own_values = [], []
    for t in range(NEW):
        fresh = r2[request * NEW + t].astype(F32)
        score = jnp.sum(row_queries * fresh[HEADS : HEADS + 1], axis=1, keepdims=True)
        score = jnp.broadcast_to(score, (HEADS, LANES))
        own_scores.append(jnp.where(t <= place, score, FLOOR_SCORE))
        own_values.append(fresh[HEADS + 1 : HEADS + 2])
    top = functools.reduce(jnp.maximum, own_scores)

    wait_bytes(r4.at[pl.ds(0, members - 1)], recv_sem.at[2])
    tops, wholes = [], []
    for j in range(members):
        both = r4[j, HEADS:, :]
        swapped = pltpu.roll(both, LANES // 2, 1)
        tops.append(jnp.where(lane_tile < LANES // 2, both, swapped))
        wholes.append(jnp.where(lane_tile < LANES // 2, swapped, both))
    top = functools.reduce(jnp.maximum, tops, top)
    mix, whole = jnp.zeros((HEADS, LANES), F32), jnp.zeros((HEADS, LANES), F32)
    for t in range(NEW):
        weight = jnp.exp2((own_scores[t] - top) * factor)
        whole = whole + weight
        mix = mix + weight * own_values[t]
    for j in range(members):
        shrink = jnp.exp2((tops[j] - top) * factor)
        whole = whole + wholes[j] * shrink
        mix = mix + r4[j, :HEADS, :] * shrink
    s5[...] = mix / whole
    own_rows = pl.ds(pl.multiple_of(me * HEADS, HEADS), HEADS)
    r5[own_rows, :] = s5[...]
    send_members(3, lambda other: s5, r5.at[own_rows])
    ready("wout")
    wait_bytes(r5.at[pl.ds(0, (members - 1) * HEADS)], recv_sem.at[3])

    attended = jnp.concatenate(
        [r5[pl.ds(h, rows, stride=HEADS), :].astype(BF16) for h in range(HEADS)], axis=1
    )
    spread(token_lines, token_f)
    share, after_f = sum_peers(
        4,
        jnp.dot(attended, wout[...], preferred_element_type=F32),
        token_lines[own_lines, :],
        s5b,
        r5b,
        s5c,
        r5c,
    )
    ready("wgate", "wup")

    scaled_mid = (after_f * gain_two[...].astype(F32)[None, :]).astype(BF16)
    square_mid = jnp.sum(after_f * after_f, axis=1, keepdims=True)
    columns = 4 * LANES
    line_ids = lax.broadcasted_iota(jnp.int32, (half, LANES), 0)
    square_code = code_of(square_mid)
    square_whole = jnp.floor(square_code)
    square_rest = jnp.floor((square_code - square_whole) * STEPS + 0.5)
    for index, (weight, staged, packed, landed) in enumerate(
        ((wgate, g6a, s6a, r6a), (wup, g6b, s6b, r6b))
    ):
        largest = jnp.zeros((rows, LANES), F32)
        for n in range(weight.shape[1] // columns):
            part = jnp.dot(
                scaled_mid,
                weight[:, n * columns : (n + 1) * columns],
                preferred_element_type=F32,
            )
            for c in range(columns // LANES):
                line = n * (columns // LANES) + c
                piece = part[:, c * LANES : (c + 1) * LANES]
                staged[pl.ds(line, rows, stride=half), :] = piece
                largest = jnp.maximum(largest, jnp.abs(piece))
        unit_code = jnp.ceil(code_of(jnp.max(largest, axis=1, keepdims=True)))
        to_steps = jnp.broadcast_to(STEPS / value_of(unit_code), (rows, LANES))
        for line, extra in enumerate((unit_code, square_whole, square_rest)):
            staged[pl.ds(chunks + line, rows, stride=half), :] = jnp.broadcast_to(
                extra, (rows, LANES)
            )
        for i in range(rows):
            line = staged[i * half : (i + 1) * half, :]
            line = jnp.where(
                line_ids < chunks, jnp.floor(line * to_steps[i : i + 1] + 0.5), line
            )
            packed[i] = line.astype(jnp.int32).astype(jnp.int16)
        landed[me] = packed[me]
        send_members(6 + index, lambda other: packed.at[other], landed.at[me])

    def add_up(landed):
        whole, square = jnp.zeros((half, LANES), F32), jnp.zeros((1, LANES), F32)
        for j in range(members):
            part = landed[j].astype(jnp.int32).astype(F32)
            codes = part[chunks : chunks + 3]
            whole = whole + part * (value_of(codes[0:1]) * (1.0 / STEPS))
            square = square + value_of(codes[1:2] + codes[2:3] * (1.0 / STEPS))
        return whole, square

    wait_bytes(r6a.at[pl.ds(0, members - 1)], recv_sem.at[6])
    gate, square = add_up(r6a)
    inverse_two = 1.0 / jnp.sqrt(square / model_width + EPSILON)
    gate = gate * inverse_two
    gate = gate / (1.0 + jnp.exp(-gate))
    wait_bytes(r6b.at[pl.ds(0, members - 1)], recv_sem.at[7])
    up, _ = add_up(r6b)
    s7[...] = (gate * (up * inverse_two)).astype(BF16)
    r7[me] = s7[...]
    send_members(8, lambda other: s7, r7.at[me])
    ready("wdown")
    wait_bytes(r7.at[pl.ds(0, members - 1)], recv_sem.at[8])

    for i in range(rows):
        g7[i * half : (i + 1) * half, :] = r7[i].astype(F32)
    down = jnp.zeros((rows, wdown.shape[1]), F32)
    for n in range(chunks // 4):
        hidden = jnp.concatenate(
            [g7[pl.ds(n * 4 + c, rows, stride=half), :].astype(BF16) for c in range(4)], axis=1
        )
        down = down + jnp.dot(
            hidden, wdown[n * 4 * LANES : (n + 1) * 4 * LANES, :], preferred_element_type=F32
        )
    _, result = sum_peers(9, down, share, s7b, r7b, s7c, r7c)
    out_ref[...] = result.astype(BF16)

    wait_bytes(r1.at[pl.ds(0, members - 1), pl.ds(0, used)], send_sem.at[0])
    wait_bytes(r2.at[pl.ds(0, members - 1)], send_sem.at[1])
    wait_bytes(r4.at[pl.ds(0, members - 1)], send_sem.at[2])
    wait_bytes(r5.at[pl.ds(0, (members - 1) * HEADS)], send_sem.at[3])
    for phase, landed, whole in ((4, r5b, r5c), (9, r7b, r7c)):
        wait_bytes(landed.at[pl.ds(0, peers - 1)], send_sem.at[phase])
        wait_bytes(whole.at[pl.ds(0, (peers - 1) * lines_own)], send_sem.at[phase + 1])
    for phase, landed in ((6, r6a), (7, r6b), (8, r7)):
        wait_bytes(landed.at[pl.ds(0, members - 1)], send_sem.at[phase])


def local(
    members,
    peers,
    tokens,
    attn_gain,
    query_key_value_weight,
    paged_key_store,
    paged_value_store,
    lengths,
    block_table,
    out_weight,
    mlp_gain,
    gate_weight,
    up_weight,
    down_weight,
):
    rows, width_part = tokens.shape
    slots, _, block_len, head_dim = paged_key_store.shape
    hidden_part = gate_weight.shape[1]
    half = (hidden_part // LANES + 3 + 15) // 16 * 16
    exponents = np.arange(head_dim // 2, dtype=np.float32) * np.float32(
        -2.0 * math.log(ROPE_BASE) / head_dim
    )
    inverse = np.exp(exponents.astype(np.float64)).astype(np.float32)
    freq = jnp.asarray(np.concatenate([inverse, inverse])[None, :])

    any_spec = pl.BlockSpec(memory_space=pl.ANY)
    vmem_spec = pl.BlockSpec(memory_space=pltpu.VMEM)
    cuts = width_part // LANES
    lines_own = rows // peers * cuts
    scratch = [
        pltpu.VMEM(tokens.shape, BF16),
        pltpu.VMEM(freq.shape, F32),
        pltpu.VMEM(block_table.shape, jnp.int32),
        pltpu.VMEM(query_key_value_weight.shape, BF16),
        pltpu.VMEM((slots, block_len, head_dim), BF16),
        pltpu.VMEM((slots, block_len, head_dim), BF16),
        pltpu.VMEM(out_weight.shape, BF16),
        pltpu.VMEM(gate_weight.shape, BF16),
        pltpu.VMEM(up_weight.shape, BF16),
        pltpu.VMEM(down_weight.shape, BF16),
        pltpu.VMEM((REQUESTS, GROUP, head_dim), BF16),
        pltpu.VMEM((8, slots), jnp.int32),
        pltpu.SMEM((8, slots), jnp.int32),
        pltpu.VMEM((REQUESTS, GROUP, LANES), F32),
        pltpu.VMEM((slots, GROUP, LANES), F32),
        pltpu.VMEM((rows * rows, LANES), F32),
        pltpu.VMEM((members, rows, LANES), F32),
        pltpu.VMEM((16, LANES), BF16),
        pltpu.VMEM((members, 16, LANES), BF16),
        pltpu.VMEM((members, 2 * HEADS, LANES), F32),
        pltpu.VMEM((members, 2 * HEADS, LANES), F32),
        pltpu.VMEM((HEADS, LANES), F32),
        pltpu.VMEM((members * HEADS, LANES), F32),
        pltpu.VMEM((rows * cuts, LANES), F32),
        pltpu.VMEM((rows * cuts, LANES), F32),
        pltpu.VMEM((peers, lines_own, LANES), F32),
        pltpu.VMEM((lines_own, LANES), F32),
        pltpu.VMEM((rows * cuts, LANES), F32),
        pltpu.VMEM((rows * half, LANES), F32),
        pltpu.VMEM((members, half, LANES), jnp.int16),
        pltpu.VMEM((members, half, LANES), jnp.int16),
        pltpu.VMEM((rows * half, LANES), F32),
        pltpu.VMEM((members, half, LANES), jnp.int16),
        pltpu.VMEM((members, half, LANES), jnp.int16),
        pltpu.VMEM((half, LANES), BF16),
        pltpu.VMEM((members, half, LANES), BF16),
        pltpu.VMEM((rows * half, LANES), F32),
        pltpu.VMEM((rows * cuts, LANES), F32),
        pltpu.VMEM((peers, lines_own, LANES), F32),
        pltpu.VMEM((lines_own, LANES), F32),
        pltpu.VMEM((rows * cuts, LANES), F32),
        pltpu.SemaphoreType.DMA,
        pltpu.SemaphoreType.DMA((3 + 6 * PIECES + 2,)),
        pltpu.SemaphoreType.DMA((11,)),
        pltpu.SemaphoreType.DMA((11,)),
    ]
    return pl.pallas_call(
        functools.partial(kernel, members, peers, width_part * members),
        out_shape=jax.ShapeDtypeStruct(tokens.shape, BF16),
        in_specs=[
            pl.BlockSpec(memory_space=pltpu.SMEM),
            any_spec,
            vmem_spec,
            vmem_spec,
        ]
        + [any_spec] * 9,
        out_specs=vmem_spec,
        scratch_shapes=scratch,
        compiler_params=pltpu.CompilerParams(
            collective_id=0, has_side_effects=True, vmem_limit_bytes=56 * 1024 * 1024
        ),
        name="decoder_layer",
    )(
        lengths,
        tokens,
        attn_gain,
        mlp_gain,
        freq,
        block_table,
        query_key_value_weight,
        paged_key_store,
        paged_value_store,
        out_weight,
        gate_weight,
        up_weight,
        down_weight,
    )


def solution(mesh):
    return jax.shard_map(
        functools.partial(local, mesh.shape["mem"], mesh.shape["mp"]),
        mesh=mesh,
        in_specs=(
            P(None, "mem"),
            P("mem"),
            P("mem", "mp"),
            P("mem", "mp", None, None),
            P("mem", "mp", None, None),
            P(),
            P(),
            P("mp", "mem"),
            P("mem"),
            P("mem", "mp"),
            P("mem", "mp"),
            P("mp", "mem"),
        ),
        out_specs=P(None, "mem"),
        check_vma=False,
    )
```

time: 448 us -> 65.2 us (0.15)
  blocking collectives: 221 us -> 0 us
  waiting for transfers between devices: 148 us -> 0 us
  Pallas kernels: 0 us -> 63.6 us
  local copies, waits for them, and re-layouts: 31.6 us -> 1.32 us
  matrix products: 17.1 us -> 0 us
  between operations: 13.9 us -> 0.01 us
  other arithmetic: 13.3 us -> 0 us
    psum x3 -> x0, waiting for transfers between devices: 148 us -> none  [the longest x1 55.3 us: local(): total, accum = lax.psum((total * shrink, accum * shrink[..., None]), 'mem')]
    psum x5 -> x0, blocking collectives: 141 us -> none  [the longest x1 35.3 us: local(): lax.psum((partial_proj, jnp.sum(token_f * token_f, axis=1)), 'mem')]
    pmax x1 -> x0, blocking collectives: 79.9 us -> none  [local(): overall = lax.pmax(best, 'mem')]
    pallas_call x0 -> x1, Pallas kernels: none -> 63.6 us  [local(): pl.pallas_call(functools.partial(kernel, members, peers, width_part * mem...]
    gather x24 -> x0, local copies, waits for them, and re-layouts: 30.4 us -> none  [the longest x3 8.51 us: visit(): block_keys = paged_key_store[picked]]
    dot_general x19 -> x0, matrix products: 17.1 us -> none  [the longest x1 3.47 us: local(): jnp.dot(scaled_mid, up_weight, preferred_element_type=jnp.float32)]
  transfers between devices with their start and end apart: 3 -> 0, of which waited for: 3 -> 0; matrix products, arithmetic and copies ran while one was open for 2% -> 0% of each run, Pallas kernels for 0% -> 0%
where the time goes in v1:
time: 65.2 us; the launch traced here: 65 us
  Pallas kernels  63.6 us (98%)
  local copies, waits for them, and re-layouts  1.32 us (2%)
    pallas_call x1, Pallas kernels, local(): pl.pallas_call(functools.partial(kernel, members, peers, width_part * mem...  63.6 us
    unnamed x1, local copies, waits for them, and re-layouts  1.32 us

profile of v1, /device:TPU:1, one launch (start us, length us, event | category | flops | bytes accessed | tf_op | source)
XLA Modules:
  0.0 65.0 jit_solution(9350569859684464046)
XLA Ops:
  0.0 63.6 %decoder_layer.1 = bf16[16,512]{1,0:T(8,128)(2,1)} custom-call(s32[4]{0:T(128)} %lengths.1, bf16[16,512]{1,0:T(8,128)(2,1)} %tokens_hbm.1, bf16[512]{0:T(512)(128)(2,1)} %gain_one.1, bf16[512]{0:T(512)(128)(2,1)} %gain_two.1, f32[1,128]{1,0:T(1,128)} %constant.2.clone.freq_hbm, s32[4,512]{1,0:T(4,128)} %table_hbm.1, bf16[512,1280]{1,0:T(8,128)(2,1)} %wqkv_hbm.1, ...), custom_call_target="tpu_custom_call" | custom-call | tf_op jit(solution)/shard_map/decoder_layer/pallas_call | solution.py:570
  63.6 1.3 %copy.15 = bf16[16,512]{1,0:T(8,128)(2,1)} copy(bf16[16,512]{1,0:T(8,128)(2,1)} %decoder_layer.1) | data formatting | bytes 32768

commit v2 on v1

--- a/solution.py
+++ b/solution.py
@@ -97,11 +97,8 @@
     r4,
     s5,
     r5,
-    token_lines,
     s5b,
     r5b,
-    s5c,
-    r5c,
     g6a,
     s6a,
     r6a,
@@ -113,8 +110,6 @@
     g7,
     s7b,
     r7b,
-    s7c,
-    r7c,
     code_sem,
     fetch_sem,
     send_sem,
@@ -172,11 +167,11 @@
                 device_id_type=MESH,
             ).start()
 
-    def send_peers(phase, source_of, target):
+    def send_peers(phase, source, target):
         for k in range(1, peers):
             other = lax.rem(mine + k, peers)
             pltpu.make_async_remote_copy(
-                src_ref=source_of(other),
+                src_ref=source,
                 dst_ref=target,
                 send_sem=send_sem.at[phase],
                 recv_sem=recv_sem.at[phase],
@@ -184,35 +179,24 @@
                 device_id_type=MESH,
             ).start()
 
-    cuts = tokens.shape[1] // LANES
-    lines_own = rows // peers * cuts
-    own_lines = pl.ds(pl.multiple_of(mine * lines_own, lines_own), lines_own)
-
-    def spread(ref, array):
-        for c in range(cuts):
-            ref[pl.ds(c, rows, stride=cuts), :] = array[:, c * LANES : (c + 1) * LANES]
-
-    def gather(ref):
-        return jnp.concatenate([ref[pl.ds(c, rows, stride=cuts), :] for c in range(cuts)], axis=1)
-
-    def sum_peers(phase, partial, residual, staged, landed, rounded, whole, between=None):
-        spread(staged, partial)
-        send_peers(
-            phase, lambda other: staged.at[pl.ds(other * lines_own, lines_own)], landed.at[mine]
+    width = tokens.shape[1]
+
+    def sum_peers(phase, partial, staged, landed):
+        unit_code = jnp.ceil(code_of(jnp.max(jnp.abs(partial), axis=1, keepdims=True)))
+        steps = jnp.floor(partial * (STEPS / value_of(unit_code)) + 0.5)
+        staged[:, :width] = steps.astype(jnp.int32).astype(jnp.int16)
+        staged[:, width:] = (
+            jnp.broadcast_to(unit_code, (rows, LANES)).astype(jnp.int32).astype(jnp.int16)
         )
-        landed[mine] = staged[own_lines, :]
-        if between is not None:
-            between()
+        send_peers(phase, staged, landed.at[mine])
+        landed[mine] = staged[...]
         wait_bytes(landed.at[pl.ds(0, peers - 1)], recv_sem.at[phase])
-        total = landed[0]
-        for j in range(1, peers):
-            total = total + landed[j]
-        share = (residual + total).astype(BF16).astype(F32)
-        rounded[...] = share
-        whole[own_lines, :] = share
-        send_peers(phase + 1, lambda other: rounded, whole.at[own_lines])
-        wait_bytes(whole.at[pl.ds(0, (peers - 1) * lines_own)], recv_sem.at[phase + 1])
-        return share, gather(whole)
+        total = jnp.zeros((rows, width), F32)
+        for j in range(peers):
+            part = landed[j].astype(jnp.int32).astype(F32)
+            unit = value_of(part[:, width:]) * (1.0 / STEPS)
+            total = total + part[:, :width] * jnp.concatenate([unit] * (width // LANES), axis=1)
+        return total
 
     def wait_bytes(window, semaphore):
         pltpu.make_async_copy(window, window, semaphore).wait()
@@ -222,8 +206,6 @@
     scaled_in = (token_f * gain_one[...].astype(F32)[None, :]).astype(BF16)
     square_one = jnp.sum(token_f * token_f, axis=1, keepdims=True)
     ready("wqkv")
-    fetch("keys", keys_hbm.at[:, 0], keys, PIECES)
-    fetch("values", values_hbm.at[:, 0], values, PIECES)
     projected = jnp.dot(scaled_in, wqkv[...], preferred_element_type=F32)
     for c in range(HEADS + 2):
         s1[pl.ds(c, rows, stride=rows), :] = projected[:, c * LANES : (c + 1) * LANES]
@@ -237,10 +219,8 @@
     )
     r1[me] = s1[pl.ds(pl.multiple_of(me * rows, rows), rows), :]
 
-    fetch("wout", wout_hbm, wout, 2)
-    fetch("wgate", wgate_hbm, wgate, PIECES)
-    fetch("wup", wup_hbm, wup, PIECES)
-    fetch("wdown", wdown_hbm, wdown, PIECES)
+    fetch("keys", keys_hbm.at[:, 0], keys, PIECES)
+    fetch("values", values_hbm.at[:, 0], values, PIECES)
 
     request, place = me // NEW, lax.rem(me, NEW)
     ready("freq")
@@ -280,6 +260,10 @@
     s2[...] = jnp.where(head_row <= HEADS, turned, total).astype(BF16)
     r2[me] = s2[...]
     send_members(1, lambda other: s2, r2.at[me])
+    fetch("wout", wout_hbm, wout, 2)
+    fetch("wgate", wgate_hbm, wgate, PIECES)
+    fetch("wup", wup_hbm, wup, PIECES)
+    fetch("wdown", wdown_hbm, wdown, PIECES)
     wait_bytes(r2.at[pl.ds(0, members - 1)], recv_sem.at[1])
 
     for r in range(REQUESTS):
@@ -395,16 +379,8 @@
     attended = jnp.concatenate(
         [r5[pl.ds(h, rows, stride=HEADS), :].astype(BF16) for h in range(HEADS)], axis=1
     )
-    spread(token_lines, token_f)
-    share, after_f = sum_peers(
-        4,
-        jnp.dot(attended, wout[...], preferred_element_type=F32),
-        token_lines[own_lines, :],
-        s5b,
-        r5b,
-        s5c,
-        r5c,
-    )
+    partial = jnp.dot(attended, wout[...], preferred_element_type=F32)
+    after_f = (token_f + sum_peers(4, partial, s5b, r5b)).astype(BF16).astype(F32)
     ready("wgate", "wup")
 
     scaled_mid = (after_f * gain_two[...].astype(F32)[None, :]).astype(BF16)
@@ -442,7 +418,7 @@
             )
             packed[i] = line.astype(jnp.int32).astype(jnp.int16)
         landed[me] = packed[me]
-        send_members(6 + index, lambda other: packed.at[other], landed.at[me])
+        send_members(5 + index, lambda other: packed.at[other], landed.at[me])
 
     def add_up(landed):
         whole, square = jnp.zeros((half, LANES), F32), jnp.zeros((1, LANES), F32)
@@ -453,18 +429,18 @@
             square = square + value_of(codes[1:2] + codes[2:3] * (1.0 / STEPS))
         return whole, square
 
-    wait_bytes(r6a.at[pl.ds(0, members - 1)], recv_sem.at[6])
+    wait_bytes(r6a.at[pl.ds(0, members - 1)], recv_sem.at[5])
     gate, square = add_up(r6a)
     inverse_two = 1.0 / jnp.sqrt(square / model_width + EPSILON)
     gate = gate * inverse_two
     gate = gate / (1.0 + jnp.exp(-gate))
-    wait_bytes(r6b.at[pl.ds(0, members - 1)], recv_sem.at[7])
+    wait_bytes(r6b.at[pl.ds(0, members - 1)], recv_sem.at[6])
     up, _ = add_up(r6b)
     s7[...] = (gate * (up * inverse_two)).astype(BF16)
     r7[me] = s7[...]
-    send_members(8, lambda other: s7, r7.at[me])
+    send_members(7, lambda other: s7, r7.at[me])
     ready("wdown")
-    wait_bytes(r7.at[pl.ds(0, members - 1)], recv_sem.at[8])
+    wait_bytes(r7.at[pl.ds(0, members - 1)], recv_sem.at[7])
 
     for i in range(rows):
         g7[i * half : (i + 1) * half, :] = r7[i].astype(F32)
@@ -476,17 +452,15 @@
         down = down + jnp.dot(
             hidden, wdown[n * 4 * LANES : (n + 1) * 4 * LANES, :], preferred_element_type=F32
         )
-    _, result = sum_peers(9, down, share, s7b, r7b, s7c, r7c)
-    out_ref[...] = result.astype(BF16)
+    out_ref[...] = (after_f + sum_peers(8, down, s7b, r7b)).astype(BF16)
 
     wait_bytes(r1.at[pl.ds(0, members - 1), pl.ds(0, used)], send_sem.at[0])
     wait_bytes(r2.at[pl.ds(0, members - 1)], send_sem.at[1])
     wait_bytes(r4.at[pl.ds(0, members - 1)], send_sem.at[2])
     wait_bytes(r5.at[pl.ds(0, (members - 1) * HEADS)], send_sem.at[3])
-    for phase, landed, whole in ((4, r5b, r5c), (9, r7b, r7c)):
+    for phase, landed in ((4, r5b), (8, r7b)):
         wait_bytes(landed.at[pl.ds(0, peers - 1)], send_sem.at[phase])
-        wait_bytes(whole.at[pl.ds(0, (peers - 1) * lines_own)], send_sem.at[phase + 1])
-    for phase, landed in ((6, r6a), (7, r6b), (8, r7)):
+    for phase, landed in ((5, r6a), (6, r6b), (7, r7)):
         wait_bytes(landed.at[pl.ds(0, members - 1)], send_sem.at[phase])
 
 
@@ -518,8 +492,6 @@
 
     any_spec = pl.BlockSpec(memory_space=pl.ANY)
     vmem_spec = pl.BlockSpec(memory_space=pltpu.VMEM)
-    cuts = width_part // LANES
-    lines_own = rows // peers * cuts
     scratch = [
         pltpu.VMEM(tokens.shape, BF16),
         pltpu.VMEM(freq.shape, F32),
@@ -544,11 +516,8 @@
         pltpu.VMEM((members, 2 * HEADS, LANES), F32),
         pltpu.VMEM((HEADS, LANES), F32),
         pltpu.VMEM((members * HEADS, LANES), F32),
-        pltpu.VMEM((rows * cuts, LANES), F32),
-        pltpu.VMEM((rows * cuts, LANES), F32),
-        pltpu.VMEM((peers, lines_own, LANES), F32),
-        pltpu.VMEM((lines_own, LANES), F32),
-        pltpu.VMEM((rows * cuts, LANES), F32),
+        pltpu.VMEM((rows, width_part + LANES), jnp.int16),
+        pltpu.VMEM((peers, rows, width_part + LANES), jnp.int16),
         pltpu.VMEM((rows * half, LANES), F32),
         pltpu.VMEM((members, half, LANES), jnp.int16),
         pltpu.VMEM((members, half, LANES), jnp.int16),
@@ -558,14 +527,12 @@
         pltpu.VMEM((half, LANES), BF16),
         pltpu.VMEM((members, half, LANES), BF16),
         pltpu.VMEM((rows * half, LANES), F32),
-        pltpu.VMEM((rows * cuts, LANES), F32),
-        pltpu.VMEM((peers, lines_own, LANES), F32),
-        pltpu.VMEM((lines_own, LANES), F32),
-        pltpu.VMEM((rows * cuts, LANES), F32),
+        pltpu.VMEM((rows, width_part + LANES), jnp.int16),
+        pltpu.VMEM((peers, rows, width_part + LANES), jnp.int16),
         pltpu.SemaphoreType.DMA,
         pltpu.SemaphoreType.DMA((3 + 6 * PIECES + 2,)),
-        pltpu.SemaphoreType.DMA((11,)),
-        pltpu.SemaphoreType.DMA((11,)),
+        pltpu.SemaphoreType.DMA((9,)),
+        pltpu.SemaphoreType.DMA((9,)),
     ]
     return pl.pallas_call(
         functools.partial(kernel, members, peers, width_part * members),

time: 65.2 us -> 59.7 us (0.916)
  Pallas kernels: 63.6 us -> 58.1 us
    pallas_call x1, Pallas kernels: 63.6 us -> 58.1 us  [local(): pl.pallas_call(functools.partial(kernel, members, peers, width_part * mem...]
where the time goes in v2:
time: 59.7 us; the launch traced here: 59.4 us
  Pallas kernels  58.1 us (97%)
  local copies, waits for them, and re-layouts  1.32 us (2%)
    pallas_call x1, Pallas kernels, local(): pl.pallas_call(functools.partial(kernel, members, peers, width_part * mem...  58.1 us
    unnamed x1, local copies, waits for them, and re-layouts  1.32 us

profile of v2, /device:TPU:1, one launch (start us, length us, event | category | flops | bytes accessed | tf_op | source)
XLA Modules:
  0.0 59.4 jit_solution(4863898334481923780)
XLA Ops:
  0.0 58.1 %decoder_layer.1 = bf16[16,512]{1,0:T(8,128)(2,1)} custom-call(s32[4]{0:T(128)} %lengths.1, bf16[16,512]{1,0:T(8,128)(2,1)} %tokens_hbm.1, bf16[512]{0:T(512)(128)(2,1)} %gain_one.1, bf16[512]{0:T(512)(128)(2,1)} %gain_two.1, f32[1,128]{1,0:T(1,128)} %constant.2.clone.freq_hbm, s32[4,512]{1,0:T(4,128)} %table_hbm.1, bf16[512,1280]{1,0:T(8,128)(2,1)} %wqkv_hbm.1, ...), custom_call_target="tpu_custom_call" | custom-call | tf_op jit(solution)/shard_map/decoder_layer/pallas_call | solution.py:537
  58.1 1.3 %copy.15 = bf16[16,512]{1,0:T(8,128)(2,1)} copy(bf16[16,512]{1,0:T(8,128)(2,1)} %decoder_layer.1) | data formatting | bytes 32768

commit v3 on v2

--- a/solution.py
+++ b/solution.py
@@ -22,7 +22,10 @@
 REQUESTS = 4
 GROUP = NEW * HEADS
 OWNER = 256
+VALUE_TILE = 8
 TILE = 16
+GROUPS = 4
+LINES = 8
 PIECES = 4
 
 HALF_PI = (1.5703125, 0.000484466552734375, -6.397578377557687e-07)
@@ -99,12 +102,9 @@
     r5,
     s5b,
     r5b,
-    g6a,
-    s6a,
-    r6a,
-    g6b,
-    s6b,
-    r6b,
+    g6,
+    s6,
+    r6,
     s7,
     r7,
     g7,
@@ -114,14 +114,13 @@
     fetch_sem,
     send_sem,
     recv_sem,
+    group_sem,
 ):
     me = lax.axis_index("mem")
     mine = lax.axis_index("mp")
     rows = tokens.shape[0]
     slots = keys.shape[0]
     block_len = keys.shape[1]
-    chunks = wgate.shape[1] // LANES
-    half = s7.shape[0]
 
     barrier = pltpu.get_barrier_semaphore()
     for k in range(1, members):
@@ -229,26 +228,6 @@
     lane_row = lax.broadcasted_iota(jnp.int32, (1, LANES), 1)
     sine = jnp.where(lane_row < LANES // 2, -sine, sine)
 
-    ready("table")
-    first_slot = me * slots
-    max_blocks = table.shape[1]
-    block_start = lax.broadcasted_iota(jnp.int32, (1, max_blocks), 1) * block_len
-    slot_ids = first_slot + lax.broadcasted_iota(jnp.int32, (slots, max_blocks), 0)
-    code = jnp.zeros((slots, max_blocks), jnp.int32)
-    for r in range(REQUESTS):
-        held = jnp.clip(lengths[r] - block_start, 0, block_len)
-        held = jnp.where(held > 0, held + r * OWNER, 0)
-        code = code + jnp.where(table[r : r + 1, :] == slot_ids, held, 0)
-    code = jnp.sum(code, axis=1, keepdims=True)
-    diagonal = lax.broadcasted_iota(jnp.int32, (slots, slots), 0) == lax.broadcasted_iota(
-        jnp.int32, (slots, slots), 1
-    )
-    code = jnp.sum(jnp.where(diagonal, code, 0), axis=0, keepdims=True)
-    owner_row = code // OWNER
-    codes[0:1, :] = code
-    to_scalars = pltpu.make_async_copy(codes, slot_codes, code_sem)
-    to_scalars.start()
-
     wait_bytes(r1.at[pl.ds(0, members - 1), pl.ds(0, used)], recv_sem.at[0])
     total = r1[0]
     for j in range(1, members):
@@ -264,6 +243,27 @@
     fetch("wgate", wgate_hbm, wgate, PIECES)
     fetch("wup", wup_hbm, wup, PIECES)
     fetch("wdown", wdown_hbm, wdown, PIECES)
+
+    ready("table")
+    first_slot = me * slots
+    max_blocks = table.shape[1]
+    block_start = lax.broadcasted_iota(jnp.int32, (1, max_blocks), 1) * block_len
+    slot_ids = first_slot + lax.broadcasted_iota(jnp.int32, (slots, max_blocks), 0)
+    code = jnp.zeros((slots, max_blocks), jnp.int32)
+    for r in range(REQUESTS):
+        held = jnp.clip(lengths[r] - block_start, 0, block_len)
+        held = jnp.where(held > 0, held + r * OWNER, 0)
+        code = code + jnp.where(table[r : r + 1, :] == slot_ids, held, 0)
+    code = jnp.sum(code, axis=1, keepdims=True)
+    diagonal = lax.broadcasted_iota(jnp.int32, (slots, slots), 0) == lax.broadcasted_iota(
+        jnp.int32, (slots, slots), 1
+    )
+    code = jnp.sum(jnp.where(diagonal, code, 0), axis=0, keepdims=True)
+    owner_row = code // OWNER
+    codes[0:1, :] = code
+    to_scalars = pltpu.make_async_copy(codes, slot_codes, code_sem)
+    to_scalars.start()
+
     wait_bytes(r2.at[pl.ds(0, members - 1)], recv_sem.at[1])
 
     for r in range(REQUESTS):
@@ -305,28 +305,31 @@
 
     def value_step(step, carry):
         sums, mixed = carry
-        line = []
-        for j in range(TILE):
-            slot = step * TILE + j
+        high_line, low_line = [], []
+        for j in range(VALUE_TILE):
+            slot = step * VALUE_TILE + j
             owner, _ = slot_of(slot)
             weight = jnp.exp2((scores[slot] - tops_ref[owner]) * factor)
             sums = jnp.where(lane_group == slot, jnp.sum(weight, axis=1, keepdims=True), sums)
-            weight = weight.astype(BF16)
-            line.append(
-                jnp.concatenate(
-                    [jnp.where(owner == r, weight, jnp.zeros_like(weight)) for r in range(REQUESTS)],
-                    axis=0,
+            high = weight.astype(BF16)
+            low = (weight - high.astype(F32)).astype(BF16)
+            for line, part in ((high_line, high), (low_line, low)):
+                line.append(
+                    jnp.concatenate(
+                        [jnp.where(owner == r, part, jnp.zeros_like(part)) for r in range(REQUESTS)],
+                        axis=0,
+                    )
                 )
-            )
-        block = values[pl.ds(step * TILE, TILE)].reshape(TILE * block_len, LANES)
-        mixed = mixed + jnp.dot(
-            jnp.concatenate(line, axis=1), block, preferred_element_type=F32
+        block = values[pl.ds(step * VALUE_TILE, VALUE_TILE)].reshape(VALUE_TILE * block_len, LANES)
+        both = jnp.concatenate(
+            [jnp.concatenate(high_line, axis=1), jnp.concatenate(low_line, axis=1)], axis=0
         )
-        return sums, mixed
+        both = jnp.dot(both, block, preferred_element_type=F32)
+        return sums, mixed + (both[: REQUESTS * GROUP] + both[REQUESTS * GROUP :])
 
     slot_sums, mixed = lax.fori_loop(
         0,
-        slots // TILE,
+        slots // VALUE_TILE,
         value_step,
         (jnp.zeros((GROUP, LANES), F32), jnp.zeros((REQUESTS * GROUP, LANES), F32)),
     )
@@ -385,82 +388,123 @@
 
     scaled_mid = (after_f * gain_two[...].astype(F32)[None, :]).astype(BF16)
     square_mid = jnp.sum(after_f * after_f, axis=1, keepdims=True)
-    columns = 4 * LANES
-    line_ids = lax.broadcasted_iota(jnp.int32, (half, LANES), 0)
     square_code = code_of(square_mid)
     square_whole = jnp.floor(square_code)
     square_rest = jnp.floor((square_code - square_whole) * STEPS + 0.5)
-    for index, (weight, staged, packed, landed) in enumerate(
-        ((wgate, g6a, s6a, r6a), (wup, g6b, s6b, r6b))
-    ):
-        largest = jnp.zeros((rows, LANES), F32)
-        for n in range(weight.shape[1] // columns):
-            part = jnp.dot(
-                scaled_mid,
-                weight[:, n * columns : (n + 1) * columns],
-                preferred_element_type=F32,
+    lane_rows = lax.broadcasted_iota(jnp.int32, (rows, LANES), 1)
+    square_line = jnp.where(lane_rows < LANES // 2, square_whole, square_rest)
+
+    quarter, group = me // GROUPS, lax.rem(me, GROUPS)
+    span = wgate.shape[1] // GROUPS
+    chunks = span // LANES
+    tall = rows * LINES
+    short = tall // GROUPS
+    for k in (2, 1, 3, 0):
+        target = lax.rem(group + k, GROUPS)
+        columns = pl.ds(pl.multiple_of(target * span, LANES), span)
+        parts = [
+            jnp.dot(scaled_mid, weight[:, columns], preferred_element_type=F32)
+            for weight in (wgate, wup)
+        ]
+        largest = jnp.maximum(jnp.abs(parts[0]), jnp.abs(parts[1]))
+        unit_code = jnp.ceil(code_of(jnp.max(largest, axis=1, keepdims=True)))
+        to_steps = STEPS / value_of(unit_code)
+        unit_line = jnp.broadcast_to(unit_code, (rows, LANES))
+        for index, (part, extra) in enumerate(zip(parts, (unit_line, square_line))):
+            base = (2 * k + index) * tall
+            steps = jnp.floor(part * to_steps + 0.5)
+            for c in range(chunks):
+                g6[pl.ds(base + c, rows, stride=LINES), :] = steps[:, c * LANES : (c + 1) * LANES]
+            g6[pl.ds(base + chunks, rows, stride=LINES), :] = extra
+            for q in range(GROUPS):
+                piece = g6[base + q * short : base + (q + 1) * short, :]
+                s6[k, q, index * short : (index + 1) * short, :] = piece.astype(jnp.int32).astype(
+                    jnp.int16
+                )
+        for j in range(1 if k == 0 else 0, GROUPS):
+            other = lax.rem(quarter + j, GROUPS)
+            pltpu.make_async_remote_copy(
+                src_ref=s6.at[k, other],
+                dst_ref=r6.at[me],
+                send_sem=send_sem.at[5],
+                recv_sem=recv_sem.at[5],
+                device_id={"mem": other * GROUPS + target},
+                device_id_type=MESH,
+            ).start()
+    r6[me] = s6[0, quarter]
+
+    wait_bytes(r6.at[pl.ds(0, members - 1)], recv_sem.at[5])
+    gates = [jnp.zeros((LINES, LANES), F32)] * GROUPS
+    ups = [jnp.zeros((LINES, LANES), F32)] * GROUPS
+    square = jnp.zeros((GROUPS, LANES), F32)
+    lane_codes = lax.broadcasted_iota(jnp.int32, (GROUPS, LANES), 1)
+    for j in range(members):
+        part = r6[j].astype(jnp.int32).astype(F32)
+        units, squares = (
+            jnp.concatenate(
+                [
+                    part[start + r * LINES + chunks : start + r * LINES + chunks + 1]
+                    for r in range(GROUPS)
+                ],
+                axis=0,
             )
-            for c in range(columns // LANES):
-                line = n * (columns // LANES) + c
-                piece = part[:, c * LANES : (c + 1) * LANES]
-                staged[pl.ds(line, rows, stride=half), :] = piece
-                largest = jnp.maximum(largest, jnp.abs(piece))
-        unit_code = jnp.ceil(code_of(jnp.max(largest, axis=1, keepdims=True)))
-        to_steps = jnp.broadcast_to(STEPS / value_of(unit_code), (rows, LANES))
-        for line, extra in enumerate((unit_code, square_whole, square_rest)):
-            staged[pl.ds(chunks + line, rows, stride=half), :] = jnp.broadcast_to(
-                extra, (rows, LANES)
-            )
-        for i in range(rows):
-            line = staged[i * half : (i + 1) * half, :]
-            line = jnp.where(
-                line_ids < chunks, jnp.floor(line * to_steps[i : i + 1] + 0.5), line
-            )
-            packed[i] = line.astype(jnp.int32).astype(jnp.int16)
-        landed[me] = packed[me]
-        send_members(5 + index, lambda other: packed.at[other], landed.at[me])
-
-    def add_up(landed):
-        whole, square = jnp.zeros((half, LANES), F32), jnp.zeros((1, LANES), F32)
-        for j in range(members):
-            part = landed[j].astype(jnp.int32).astype(F32)
-            codes = part[chunks : chunks + 3]
-            whole = whole + part * (value_of(codes[0:1]) * (1.0 / STEPS))
-            square = square + value_of(codes[1:2] + codes[2:3] * (1.0 / STEPS))
-        return whole, square
-
-    wait_bytes(r6a.at[pl.ds(0, members - 1)], recv_sem.at[5])
-    gate, square = add_up(r6a)
+            for start in (0, short)
+        )
+        units = value_of(units) * (1.0 / STEPS)
+        squares = jnp.where(lane_codes < LANES // 2, squares, squares * (1.0 / STEPS))
+        square = square + value_of(squares + pltpu.roll(squares, LANES // 2, 1))
+        for r in range(GROUPS):
+            own = slice(r * LINES, (r + 1) * LINES)
+            gates[r] = gates[r] + part[:short][own] * units[r : r + 1]
+            ups[r] = ups[r] + part[short:][own] * units[r : r + 1]
     inverse_two = 1.0 / jnp.sqrt(square / model_width + EPSILON)
-    gate = gate * inverse_two
-    gate = gate / (1.0 + jnp.exp(-gate))
-    wait_bytes(r6b.at[pl.ds(0, members - 1)], recv_sem.at[6])
-    up, _ = add_up(r6b)
-    s7[...] = (gate * (up * inverse_two)).astype(BF16)
+    hidden = []
+    for r in range(GROUPS):
+        gate = gates[r] * inverse_two[r : r + 1]
+        hidden.append(gate / (1.0 + jnp.exp(-gate)) * (ups[r] * inverse_two[r : r + 1]))
+    s7[...] = jnp.concatenate(hidden, axis=0).astype(BF16)
     r7[me] = s7[...]
-    send_members(7, lambda other: s7, r7.at[me])
+    for k in range(1, members):
+        other = lax.rem(me + k, members)
+        pltpu.make_async_remote_copy(
+            src_ref=s7,
+            dst_ref=r7.at[me],
+            send_sem=send_sem.at[6],
+            recv_sem=group_sem.at[group],
+            device_id={"mem": other},
+            device_id_type=MESH,
+        ).start()
     ready("wdown")
-    wait_bytes(r7.at[pl.ds(0, members - 1)], recv_sem.at[7])
-
-    for i in range(rows):
-        g7[i * half : (i + 1) * half, :] = r7[i].astype(F32)
+
     down = jnp.zeros((rows, wdown.shape[1]), F32)
-    for n in range(chunks // 4):
-        hidden = jnp.concatenate(
-            [g7[pl.ds(n * 4 + c, rows, stride=half), :].astype(BF16) for c in range(4)], axis=1
+    for k in (0, 1, 3, 2):
+        source = lax.rem(group + k, GROUPS)
+        arriving = GROUPS - 1 if k == 0 else GROUPS
+        wait_bytes(r7.at[pl.ds(0, arriving)], group_sem.at[source])
+        for q in range(GROUPS):
+            line = k * tall + q * short
+            g7[line : line + short, :] = r7[q * GROUPS + source].astype(F32)
+        piece = jnp.concatenate(
+            [
+                g7[pl.ds(k * tall + c, rows, stride=LINES), :].astype(BF16)
+                for c in range(chunks)
+            ],
+            axis=1,
         )
         down = down + jnp.dot(
-            hidden, wdown[n * 4 * LANES : (n + 1) * 4 * LANES, :], preferred_element_type=F32
+            piece,
+            wdown[pl.ds(pl.multiple_of(source * span, LANES), span), :],
+            preferred_element_type=F32,
         )
-    out_ref[...] = (after_f + sum_peers(8, down, s7b, r7b)).astype(BF16)
+    out_ref[...] = (after_f + sum_peers(7, down, s7b, r7b)).astype(BF16)
 
     wait_bytes(r1.at[pl.ds(0, members - 1), pl.ds(0, used)], send_sem.at[0])
     wait_bytes(r2.at[pl.ds(0, members - 1)], send_sem.at[1])
     wait_bytes(r4.at[pl.ds(0, members - 1)], send_sem.at[2])
     wait_bytes(r5.at[pl.ds(0, (members - 1) * HEADS)], send_sem.at[3])
-    for phase, landed in ((4, r5b), (8, r7b)):
+    for phase, landed in ((4, r5b), (7, r7b)):
         wait_bytes(landed.at[pl.ds(0, peers - 1)], send_sem.at[phase])
-    for phase, landed in ((5, r6a), (6, r6b), (7, r7)):
+    for phase, landed in ((5, r6), (6, r7)):
         wait_bytes(landed.at[pl.ds(0, members - 1)], send_sem.at[phase])
 
 
@@ -482,8 +526,7 @@
 ):
     rows, width_part = tokens.shape
     slots, _, block_len, head_dim = paged_key_store.shape
-    hidden_part = gate_weight.shape[1]
-    half = (hidden_part // LANES + 3 + 15) // 16 * 16
+    short = rows * LINES // GROUPS
     exponents = np.arange(head_dim // 2, dtype=np.float32) * np.float32(
         -2.0 * math.log(ROPE_BASE) / head_dim
     )
@@ -518,21 +561,19 @@
         pltpu.VMEM((members * HEADS, LANES), F32),
         pltpu.VMEM((rows, width_part + LANES), jnp.int16),
         pltpu.VMEM((peers, rows, width_part + LANES), jnp.int16),
-        pltpu.VMEM((rows * half, LANES), F32),
-        pltpu.VMEM((members, half, LANES), jnp.int16),
-        pltpu.VMEM((members, half, LANES), jnp.int16),
-        pltpu.VMEM((rows * half, LANES), F32),
-        pltpu.VMEM((members, half, LANES), jnp.int16),
-        pltpu.VMEM((members, half, LANES), jnp.int16),
-        pltpu.VMEM((half, LANES), BF16),
-        pltpu.VMEM((members, half, LANES), BF16),
-        pltpu.VMEM((rows * half, LANES), F32),
+        pltpu.VMEM((2 * GROUPS * rows * LINES, LANES), F32),
+        pltpu.VMEM((GROUPS, GROUPS, 2 * short, LANES), jnp.int16),
+        pltpu.VMEM((members, 2 * short, LANES), jnp.int16),
+        pltpu.VMEM((short, LANES), BF16),
+        pltpu.VMEM((members, short, LANES), BF16),
+        pltpu.VMEM((GROUPS * rows * LINES, LANES), F32),
         pltpu.VMEM((rows, width_part + LANES), jnp.int16),
         pltpu.VMEM((peers, rows, width_part + LANES), jnp.int16),
         pltpu.SemaphoreType.DMA,
         pltpu.SemaphoreType.DMA((3 + 6 * PIECES + 2,)),
-        pltpu.SemaphoreType.DMA((9,)),
-        pltpu.SemaphoreType.DMA((9,)),
+        pltpu.SemaphoreType.DMA((8,)),
+        pltpu.SemaphoreType.DMA((8,)),
+        pltpu.SemaphoreType.DMA((GROUPS,)),
     ]
     return pl.pallas_call(
         functools.partial(kernel, members, peers, width_part * members),

time: 59.7 us -> 61.5 us (1.030)
  Pallas kernels: 58.1 us -> 59.9 us
    pallas_call x1, Pallas kernels: 58.1 us -> 59.9 us  [local(): pl.pallas_call(functools.partial(kernel, members, peers, width_part * mem...]
where the time goes in v3:
time: 61.5 us; the launch traced here: 61.2 us
  Pallas kernels  59.9 us (97%)
  local copies, waits for them, and re-layouts  1.32 us (2%)
    pallas_call x1, Pallas kernels, local(): pl.pallas_call(functools.partial(kernel, members, peers, width_part * mem...  59.9 us
    unnamed x1, local copies, waits for them, and re-layouts  1.32 us

profile of v3, /device:TPU:1, one launch (start us, length us, event | category | flops | bytes accessed | tf_op | source)
XLA Modules:
  0.0 61.2 jit_solution(9801092223721734452)
XLA Ops:
  0.0 59.9 %decoder_layer.1 = bf16[16,512]{1,0:T(8,128)(2,1)} custom-call(s32[4]{0:T(128)} %lengths.1, bf16[16,512]{1,0:T(8,128)(2,1)} %tokens_hbm.1, bf16[512]{0:T(512)(128)(2,1)} %gain_one.1, bf16[512]{0:T(512)(128)(2,1)} %gain_two.1, f32[1,128]{1,0:T(1,128)} %constant.2.clone.freq_hbm, s32[4,512]{1,0:T(4,128)} %table_hbm.1, bf16[512,1280]{1,0:T(8,128)(2,1)} %wqkv_hbm.1, ...), custom_call_target="tpu_custom_call" | custom-call | tf_op jit(solution)/shard_map/decoder_layer/pallas_call | solution.py:578
  59.9 1.3 %copy.15 = bf16[16,512]{1,0:T(8,128)(2,1)} copy(bf16[16,512]{1,0:T(8,128)(2,1)} %decoder_layer.1) | data formatting | bytes 32768

commit v4 on v3

--- a/solution.py
+++ b/solution.py
@@ -22,7 +22,6 @@
 REQUESTS = 4
 GROUP = NEW * HEADS
 OWNER = 256
-VALUE_TILE = 8
 TILE = 16
 GROUPS = 4
 LINES = 8
@@ -63,10 +62,10 @@
     members,
     peers,
     model_width,
-    lengths,
+    lengths_hbm,
     tokens_hbm,
-    gain_one,
-    gain_two,
+    gain_one_hbm,
+    gain_two_hbm,
     freq_hbm,
     table_hbm,
     wqkv_hbm,
@@ -77,7 +76,10 @@
     wup_hbm,
     wdown_hbm,
     out_ref,
+    lengths,
     tokens,
+    gain_one,
+    gain_two,
     freq,
     table,
     wqkv,
@@ -122,15 +124,21 @@
     slots = keys.shape[0]
     block_len = keys.shape[1]
 
-    barrier = pltpu.get_barrier_semaphore()
-    for k in range(1, members):
-        pl.semaphore_signal(
-            barrier, inc=1, device_id={"mem": lax.rem(me + k, members)}, device_id_type=MESH
-        )
-    for k in range(1, peers):
-        pl.semaphore_signal(
-            barrier, inc=1, device_id={"mp": lax.rem(mine + k, peers)}, device_id_type=MESH
-        )
+    side = math.isqrt(members)
+    z, x = me // side, lax.rem(me, side)
+    steps_of = lambda d, n: min(d, n - d)
+    offsets = sorted(
+        ((dz, dx) for dz in range(side) for dx in range(side) if dz or dx),
+        key=lambda d: -steps_of(d[0], side) - steps_of(d[1], side),
+    )
+    member_order = [lax.rem(z + dz, side) * side + lax.rem(x + dx, side) for dz, dx in offsets]
+    ring, cores = peers // 2, 2
+    y, core = mine // cores, lax.rem(mine, cores)
+    offsets = sorted(
+        ((dy, dc) for dy in range(ring) for dc in range(cores) if dy or dc),
+        key=lambda d: -steps_of(d[0], ring),
+    )
+    peer_order = [lax.rem(y + dy, ring) * cores + lax.rem(core + dc, cores) for dy, dc in offsets]
 
     fetched = {}
 
@@ -139,8 +147,11 @@
         fetched[name] = []
         for p in range(pieces):
             index = sum(len(v) for v in fetched.values())
-            part = pl.ds(p * size, size)
-            copy = pltpu.make_async_copy(source.at[part], target.at[part], fetch_sem.at[index])
+            if pieces > 1:
+                part = pl.ds(p * size, size)
+                copy = pltpu.make_async_copy(source.at[part], target.at[part], fetch_sem.at[index])
+            else:
+                copy = pltpu.make_async_copy(source, target, fetch_sem.at[index])
             copy.start()
             fetched[name].append(copy)
 
@@ -150,13 +161,22 @@
                 copy.wait()
 
     fetch("tokens", tokens_hbm, tokens)
+    fetch("gain_one", gain_one_hbm, gain_one)
     fetch("wqkv", wqkv_hbm, wqkv, PIECES)
+
+    barrier = pltpu.get_barrier_semaphore()
+    for other in member_order:
+        pl.semaphore_signal(barrier, inc=1, device_id={"mem": other}, device_id_type=MESH)
+    for other in peer_order:
+        pl.semaphore_signal(barrier, inc=1, device_id={"mp": other}, device_id_type=MESH)
+
+    fetch("lengths", lengths_hbm, lengths)
+    fetch("freq", freq_hbm, freq)
     fetch("table", table_hbm, table)
-    fetch("freq", freq_hbm, freq)
+    fetch("gain_two", gain_two_hbm, gain_two)
 
     def send_members(phase, source_of, target):
-        for k in range(1, members):
-            other = lax.rem(me + k, members)
+        for other in member_order:
             pltpu.make_async_remote_copy(
                 src_ref=source_of(other),
                 dst_ref=target,
@@ -167,8 +187,7 @@
             ).start()
 
     def send_peers(phase, source, target):
-        for k in range(1, peers):
-            other = lax.rem(mine + k, peers)
+        for other in peer_order:
             pltpu.make_async_remote_copy(
                 src_ref=source,
                 dst_ref=target,
@@ -200,7 +219,7 @@
     def wait_bytes(window, semaphore):
         pltpu.make_async_copy(window, window, semaphore).wait()
 
-    ready("tokens")
+    ready("tokens", "gain_one")
     token_f = tokens[...].astype(F32)
     scaled_in = (token_f * gain_one[...].astype(F32)[None, :]).astype(BF16)
     square_one = jnp.sum(token_f * token_f, axis=1, keepdims=True)
@@ -222,7 +241,7 @@
     fetch("values", values_hbm.at[:, 0], values, PIECES)
 
     request, place = me // NEW, lax.rem(me, NEW)
-    ready("freq")
+    ready("lengths", "freq")
     position = (lengths[request] + place).astype(F32)
     sine, cosine = sine_cosine(position * freq[...])
     lane_row = lax.broadcasted_iota(jnp.int32, (1, LANES), 1)
@@ -304,35 +323,24 @@
     ready("values")
 
     def value_step(step, carry):
-        sums, mixed = carry
-        high_line, low_line = [], []
-        for j in range(VALUE_TILE):
-            slot = step * VALUE_TILE + j
+        sums, mixed = carry[0], list(carry[1])
+        for j in range(TILE):
+            slot = step * TILE + j
             owner, _ = slot_of(slot)
             weight = jnp.exp2((scores[slot] - tops_ref[owner]) * factor)
             sums = jnp.where(lane_group == slot, jnp.sum(weight, axis=1, keepdims=True), sums)
             high = weight.astype(BF16)
             low = (weight - high.astype(F32)).astype(BF16)
-            for line, part in ((high_line, high), (low_line, low)):
-                line.append(
-                    jnp.concatenate(
-                        [jnp.where(owner == r, part, jnp.zeros_like(part)) for r in range(REQUESTS)],
-                        axis=0,
-                    )
-                )
-        block = values[pl.ds(step * VALUE_TILE, VALUE_TILE)].reshape(VALUE_TILE * block_len, LANES)
-        both = jnp.concatenate(
-            [jnp.concatenate(high_line, axis=1), jnp.concatenate(low_line, axis=1)], axis=0
-        )
-        both = jnp.dot(both, block, preferred_element_type=F32)
-        return sums, mixed + (both[: REQUESTS * GROUP] + both[REQUESTS * GROUP :])
-
-    slot_sums, mixed = lax.fori_loop(
-        0,
-        slots // VALUE_TILE,
-        value_step,
-        (jnp.zeros((GROUP, LANES), F32), jnp.zeros((REQUESTS * GROUP, LANES), F32)),
-    )
+            both = jnp.dot(
+                jnp.concatenate([high, low], axis=0), values[slot], preferred_element_type=F32
+            )
+            both = both[:GROUP] + both[GROUP:]
+            for r in range(REQUESTS):
+                mixed[r] = mixed[r] + jnp.where(owner == r, both, 0.0)
+        return sums, tuple(mixed)
+
+    zero = jnp.zeros((GROUP, LANES), F32)
+    slot_sums, mixed = lax.fori_loop(0, slots // TILE, value_step, (zero, (zero,) * REQUESTS))
     lane_tile = lax.broadcasted_iota(jnp.int32, (HEADS, LANES), 1)
     for r in range(REQUESTS):
         own = jnp.where(owner_row == r, slot_sums, 0.0)
@@ -340,7 +348,7 @@
         for t in range(NEW):
             part = slice(t * HEADS, (t + 1) * HEADS)
             i = r * NEW + t
-            s4[i, :HEADS, :] = mixed[i * HEADS : (i + 1) * HEADS]
+            s4[i, :HEADS, :] = mixed[r][part]
             s4[i, HEADS:, :] = jnp.where(lane_tile < LANES // 2, best[r][part], whole[part])
     send_members(2, lambda other: s4.at[other], r4.at[me])
     r4[me] = s4[me]
@@ -384,7 +392,7 @@
     )
     partial = jnp.dot(attended, wout[...], preferred_element_type=F32)
     after_f = (token_f + sum_peers(4, partial, s5b, r5b)).astype(BF16).astype(F32)
-    ready("wgate", "wup")
+    ready("gain_two", "wgate", "wup")
 
     scaled_mid = (after_f * gain_two[...].astype(F32)[None, :]).astype(BF16)
     square_mid = jnp.sum(after_f * after_f, axis=1, keepdims=True)
@@ -399,13 +407,16 @@
     chunks = span // LANES
     tall = rows * LINES
     short = tall // GROUPS
-    for k in (2, 1, 3, 0):
-        target = lax.rem(group + k, GROUPS)
-        columns = pl.ds(pl.multiple_of(target * span, LANES), span)
-        parts = [
+
+    def multiply(k):
+        columns = pl.ds(pl.multiple_of(lax.rem(group + k, GROUPS) * span, LANES), span)
+        return [
             jnp.dot(scaled_mid, weight[:, columns], preferred_element_type=F32)
             for weight in (wgate, wup)
         ]
+
+    def ship(k, parts):
+        target = lax.rem(group + k, GROUPS)
         largest = jnp.maximum(jnp.abs(parts[0]), jnp.abs(parts[1]))
         unit_code = jnp.ceil(code_of(jnp.max(largest, axis=1, keepdims=True)))
         to_steps = STEPS / value_of(unit_code)
@@ -421,7 +432,7 @@
                 s6[k, q, index * short : (index + 1) * short, :] = piece.astype(jnp.int32).astype(
                     jnp.int16
                 )
-        for j in range(1 if k == 0 else 0, GROUPS):
+        for j in (2, 1, 3, 0) if k else (2, 1, 3):
             other = lax.rem(quarter + j, GROUPS)
             pltpu.make_async_remote_copy(
                 src_ref=s6.at[k, other],
@@ -431,6 +442,13 @@
                 device_id={"mem": other * GROUPS + target},
                 device_id_type=MESH,
             ).start()
+
+    order = (2, 1, 3, 0)
+    parts = multiply(order[0])
+    for index, k in enumerate(order):
+        later = multiply(order[index + 1]) if index + 1 < GROUPS else None
+        ship(k, parts)
+        parts = later
     r6[me] = s6[0, quarter]
 
     wait_bytes(r6.at[pl.ds(0, members - 1)], recv_sem.at[5])
@@ -464,8 +482,7 @@
         hidden.append(gate / (1.0 + jnp.exp(-gate)) * (ups[r] * inverse_two[r : r + 1]))
     s7[...] = jnp.concatenate(hidden, axis=0).astype(BF16)
     r7[me] = s7[...]
-    for k in range(1, members):
-        other = lax.rem(me + k, members)
+    for other in member_order:
         pltpu.make_async_remote_copy(
             src_ref=s7,
             dst_ref=r7.at[me],
@@ -536,7 +553,10 @@
     any_spec = pl.BlockSpec(memory_space=pl.ANY)
     vmem_spec = pl.BlockSpec(memory_space=pltpu.VMEM)
     scratch = [
+        pltpu.SMEM(lengths.shape, jnp.int32),
         pltpu.VMEM(tokens.shape, BF16),
+        pltpu.VMEM(attn_gain.shape, BF16),
+        pltpu.VMEM(mlp_gain.shape, BF16),
         pltpu.VMEM(freq.shape, F32),
         pltpu.VMEM(block_table.shape, jnp.int32),
         pltpu.VMEM(query_key_value_weight.shape, BF16),
@@ -570,7 +590,7 @@
         pltpu.VMEM((rows, width_part + LANES), jnp.int16),
         pltpu.VMEM((peers, rows, width_part + LANES), jnp.int16),
         pltpu.SemaphoreType.DMA,
-        pltpu.SemaphoreType.DMA((3 + 6 * PIECES + 2,)),
+        pltpu.SemaphoreType.DMA((6 + 6 * PIECES + 2,)),
         pltpu.SemaphoreType.DMA((8,)),
         pltpu.SemaphoreType.DMA((8,)),
         pltpu.SemaphoreType.DMA((GROUPS,)),
@@ -578,13 +598,7 @@
     return pl.pallas_call(
         functools.partial(kernel, members, peers, width_part * members),
         out_shape=jax.ShapeDtypeStruct(tokens.shape, BF16),
-        in_specs=[
-            pl.BlockSpec(memory_space=pltpu.SMEM),
-            any_spec,
-            vmem_spec,
-            vmem_spec,
-        ]
-        + [any_spec] * 9,
+        in_specs=[any_spec] * 13,
         out_specs=vmem_spec,
         scratch_shapes=scratch,
         compiler_params=pltpu.CompilerParams(

time: 61.5 us -> 56.3 us (0.915)
  Pallas kernels: 59.9 us -> 54.7 us
    pallas_call x1, Pallas kernels: 59.9 us -> 54.7 us  [local(): pl.pallas_call(functools.partial(kernel, members, peers, width_part * mem...]
where the time goes in v4:
time: 56.3 us; the launch traced here: 56 us
  Pallas kernels  54.7 us (97%)
  local copies, waits for them, and re-layouts  1.32 us (2%)
    pallas_call x1, Pallas kernels, local(): pl.pallas_call(functools.partial(kernel, members, peers, width_part * mem...  54.7 us
    unnamed x1, local copies, waits for them, and re-layouts  1.32 us

profile of v4, /device:TPU:1, one launch (start us, length us, event | category | flops | bytes accessed | tf_op | source)
XLA Modules:
  0.0 56.0 jit_solution(2670940344336512167)
XLA Ops:
  0.0 54.7 %decoder_layer.1 = bf16[16,512]{1,0:T(8,128)(2,1)} custom-call(s32[4]{0:T(128)} %lengths_hbm.1, bf16[16,512]{1,0:T(8,128)(2,1)} %tokens_hbm.1, bf16[512]{0:T(512)(128)(2,1)} %gain_one_hbm.1, bf16[512]{0:T(512)(128)(2,1)} %gain_two_hbm.1, f32[1,128]{1,0:T(1,128)} %constant.2.clone.freq_hbm, s32[4,512]{1,0:T(4,128)} %table_hbm.1, bf16[512,1280]{1,0:T(8,128)(2,1)} %wqkv_hbm.1, ...), custom_call_target="tpu_custom_call" | custom-call | tf_op jit(solution)/shard_map/decoder_layer/pallas_call | solution.py:598
  54.7 1.3 %copy.15 = bf16[16,512]{1,0:T(8,128)(2,1)} copy(bf16[16,512]{1,0:T(8,128)(2,1)} %decoder_layer.1) | data formatting | bytes 32768

commit v5 on v4

--- a/solution.py
+++ b/solution.py
@@ -22,7 +22,8 @@
 REQUESTS = 4
 GROUP = NEW * HEADS
 OWNER = 256
-TILE = 16
+TILE = 32
+PARTIAL = 16
 GROUPS = 4
 LINES = 8
 PIECES = 4
@@ -116,6 +117,7 @@
     fetch_sem,
     send_sem,
     recv_sem,
+    quarter_sem,
     group_sem,
 ):
     me = lax.axis_index("mem")
@@ -341,17 +343,33 @@
 
     zero = jnp.zeros((GROUP, LANES), F32)
     slot_sums, mixed = lax.fori_loop(0, slots // TILE, value_step, (zero, (zero,) * REQUESTS))
-    lane_tile = lax.broadcasted_iota(jnp.int32, (HEADS, LANES), 1)
+    lane_head = lax.broadcasted_iota(jnp.int32, (HEADS, LANES), 1) // (LANES // HEADS)
+    by_head = lane_head == lax.broadcasted_iota(jnp.int32, (HEADS, LANES), 0)
+
+    def to_line(column):
+        return jnp.sum(jnp.where(by_head, column, 0.0), axis=0, keepdims=True)
+
+    def to_column(line):
+        column = jnp.max(jnp.where(by_head, line, -jnp.inf), axis=1, keepdims=True)
+        return jnp.broadcast_to(column, (HEADS, LANES))
+
     for r in range(REQUESTS):
         own = jnp.where(owner_row == r, slot_sums, 0.0)
         whole = jnp.broadcast_to(jnp.sum(own, axis=1, keepdims=True), (GROUP, LANES))
         for t in range(NEW):
             part = slice(t * HEADS, (t + 1) * HEADS)
-            i = r * NEW + t
-            s4[i, :HEADS, :] = mixed[r][part]
-            s4[i, HEADS:, :] = jnp.where(lane_tile < LANES // 2, best[r][part], whole[part])
-    send_members(2, lambda other: s4.at[other], r4.at[me])
-    r4[me] = s4[me]
+            line = (r * NEW + t) * PARTIAL
+            s4[line : line + HEADS, :] = mixed[r][part]
+            s4[line + HEADS : line + HEADS + 1, :] = to_line(best[r][part])
+            s4[line + HEADS + 1 : line + HEADS + 2, :] = to_line(whole[part])
+    mine_4 = pl.ds(pl.multiple_of(me * PARTIAL, PARTIAL), PARTIAL)
+    sent = HEADS + 2
+    send_members(
+        2,
+        lambda other: s4.at[pl.ds(other * PARTIAL, sent)],
+        r4.at[pl.ds(me * PARTIAL, sent)],
+    )
+    r4[mine_4, :] = s4[mine_4, :]
 
     row_queries = r2[me].astype(F32)[:HEADS]
     own_scores, own_values = [], []
@@ -361,25 +379,22 @@
         score = jnp.broadcast_to(score, (HEADS, LANES))
         own_scores.append(jnp.where(t <= place, score, FLOOR_SCORE))
         own_values.append(fresh[HEADS + 1 : HEADS + 2])
-    top = functools.reduce(jnp.maximum, own_scores)
-
-    wait_bytes(r4.at[pl.ds(0, members - 1)], recv_sem.at[2])
-    tops, wholes = [], []
-    for j in range(members):
-        both = r4[j, HEADS:, :]
-        swapped = pltpu.roll(both, LANES // 2, 1)
-        tops.append(jnp.where(lane_tile < LANES // 2, both, swapped))
-        wholes.append(jnp.where(lane_tile < LANES // 2, swapped, both))
-    top = functools.reduce(jnp.maximum, tops, top)
-    mix, whole = jnp.zeros((HEADS, LANES), F32), jnp.zeros((HEADS, LANES), F32)
+    top = to_line(functools.reduce(jnp.maximum, own_scores))
+
+    wait_bytes(r4.at[pl.ds(0, (members - 1) * sent)], recv_sem.at[2])
+    tops = r4[pl.ds(HEADS, members, stride=PARTIAL), :]
+    wholes = r4[pl.ds(HEADS + 1, members, stride=PARTIAL), :]
+    top = jnp.maximum(top, jnp.max(tops, axis=0, keepdims=True))
+    shrink = jnp.exp2((tops - top) * factor)
+    whole = to_column(jnp.sum(wholes * shrink, axis=0, keepdims=True))
+    top = to_column(top)
+    mix = jnp.zeros((HEADS, LANES), F32)
     for t in range(NEW):
         weight = jnp.exp2((own_scores[t] - top) * factor)
         whole = whole + weight
         mix = mix + weight * own_values[t]
     for j in range(members):
-        shrink = jnp.exp2((tops[j] - top) * factor)
-        whole = whole + wholes[j] * shrink
-        mix = mix + r4[j, :HEADS, :] * shrink
+        mix = mix + r4[j * PARTIAL : j * PARTIAL + HEADS, :] * to_column(shrink[j : j + 1])
     s5[...] = mix / whole
     own_rows = pl.ds(pl.multiple_of(me * HEADS, HEADS), HEADS)
     r5[own_rows, :] = s5[...]
@@ -438,7 +453,7 @@
                 src_ref=s6.at[k, other],
                 dst_ref=r6.at[me],
                 send_sem=send_sem.at[5],
-                recv_sem=recv_sem.at[5],
+                recv_sem=quarter_sem.at[k],
                 device_id={"mem": other * GROUPS + target},
                 device_id_type=MESH,
             ).start()
@@ -451,13 +466,16 @@
         parts = later
     r6[me] = s6[0, quarter]
 
-    wait_bytes(r6.at[pl.ds(0, members - 1)], recv_sem.at[5])
     gates = [jnp.zeros((LINES, LANES), F32)] * GROUPS
     ups = [jnp.zeros((LINES, LANES), F32)] * GROUPS
     square = jnp.zeros((GROUPS, LANES), F32)
     lane_codes = lax.broadcasted_iota(jnp.int32, (GROUPS, LANES), 1)
-    for j in range(members):
-        part = r6[j].astype(jnp.int32).astype(F32)
+    for k, q in [(k, q) for k in order for q in range(GROUPS)]:
+        if q == 0:
+            arriving = GROUPS if k else GROUPS - 1
+            wait_bytes(r6.at[pl.ds(0, arriving)], quarter_sem.at[k])
+        sender = q * GROUPS + lax.rem(group + GROUPS - k, GROUPS)
+        part = r6[sender].astype(jnp.int32).astype(F32)
         units, squares = (
             jnp.concatenate(
                 [
@@ -517,7 +535,7 @@
 
     wait_bytes(r1.at[pl.ds(0, members - 1), pl.ds(0, used)], send_sem.at[0])
     wait_bytes(r2.at[pl.ds(0, members - 1)], send_sem.at[1])
-    wait_bytes(r4.at[pl.ds(0, members - 1)], send_sem.at[2])
+    wait_bytes(r4.at[pl.ds(0, (members - 1) * sent)], send_sem.at[2])
     wait_bytes(r5.at[pl.ds(0, (members - 1) * HEADS)], send_sem.at[3])
     for phase, landed in ((4, r5b), (7, r7b)):
         wait_bytes(landed.at[pl.ds(0, peers - 1)], send_sem.at[phase])
@@ -575,8 +593,8 @@
         pltpu.VMEM((members, rows, LANES), F32),
         pltpu.VMEM((16, LANES), BF16),
         pltpu.VMEM((members, 16, LANES), BF16),
-        pltpu.VMEM((members, 2 * HEADS, LANES), F32),
-        pltpu.VMEM((members, 2 * HEADS, LANES), F32),
+        pltpu.VMEM((members * PARTIAL, LANES), F32),
+        pltpu.VMEM((members * PARTIAL, LANES), F32),
         pltpu.VMEM((HEADS, LANES), F32),
         pltpu.VMEM((members * HEADS, LANES), F32),
         pltpu.VMEM((rows, width_part + LANES), jnp.int16),
@@ -593,6 +611,7 @@
         pltpu.SemaphoreType.DMA((6 + 6 * PIECES + 2,)),
         pltpu.SemaphoreType.DMA((8,)),
         pltpu.SemaphoreType.DMA((8,)),
+        pltpu.SemaphoreType.DMA((GROUPS,)),
         pltpu.SemaphoreType.DMA((GROUPS,)),
     ]
     return pl.pallas_call(

time: 56.3 us -> 55 us (0.977)
  Pallas kernels: 54.7 us -> 53.4 us
    pallas_call x1, Pallas kernels: 54.7 us -> 53.4 us  [local(): pl.pallas_call(functools.partial(kernel, members, peers, width_part * mem...]
where the time goes in v5:
time: 55 us; the launch traced here: 54.8 us
  Pallas kernels  53.4 us (97%)
  local copies, waits for them, and re-layouts  1.32 us (2%)
    pallas_call x1, Pallas kernels, local(): pl.pallas_call(functools.partial(kernel, members, peers, width_part * mem...  53.4 us
    unnamed x1, local copies, waits for them, and re-layouts  1.32 us

profile of v5, /device:TPU:1, one launch (start us, length us, event | category | flops | bytes accessed | tf_op | source)
XLA Modules:
  0.0 54.8 jit_solution(4870432867266671713)
XLA Ops:
  0.0 53.4 %decoder_layer.1 = bf16[16,512]{1,0:T(8,128)(2,1)} custom-call(s32[4]{0:T(128)} %lengths_hbm.1, bf16[16,512]{1,0:T(8,128)(2,1)} %tokens_hbm.1, bf16[512]{0:T(512)(128)(2,1)} %gain_one_hbm.1, bf16[512]{0:T(512)(128)(2,1)} %gain_two_hbm.1, f32[1,128]{1,0:T(1,128)} %constant.2.clone.freq_hbm, s32[4,512]{1,0:T(4,128)} %table_hbm.1, bf16[512,1280]{1,0:T(8,128)(2,1)} %wqkv_hbm.1, ...), custom_call_target="tpu_custom_call" | custom-call | tf_op jit(solution)/shard_map/decoder_layer/pallas_call | solution.py:617
  53.4 1.3 %copy.15 = bf16[16,512]{1,0:T(8,128)(2,1)} copy(bf16[16,512]{1,0:T(8,128)(2,1)} %decoder_layer.1) | data formatting | bytes 32768

commit v6 on v5

--- a/solution.py
+++ b/solution.py
@@ -105,6 +105,8 @@
     r5,
     s5b,
     r5b,
+    s5c,
+    r5c,
     g6,
     s6,
     r6,
@@ -113,6 +115,8 @@
     g7,
     s7b,
     r7b,
+    s7c,
+    r7c,
     code_sem,
     fetch_sem,
     send_sem,
@@ -136,11 +140,8 @@
     member_order = [lax.rem(z + dz, side) * side + lax.rem(x + dx, side) for dz, dx in offsets]
     ring, cores = peers // 2, 2
     y, core = mine // cores, lax.rem(mine, cores)
-    offsets = sorted(
-        ((dy, dc) for dy in range(ring) for dc in range(cores) if dy or dc),
-        key=lambda d: -steps_of(d[0], ring),
-    )
-    peer_order = [lax.rem(y + dy, ring) * cores + lax.rem(core + dc, cores) for dy, dc in offsets]
+    peer_order = [lax.rem(y + dy, ring) * cores + core for dy in (ring // 2, 1, ring - 1)]
+    partner = y * cores + 1 - core
 
     fetched = {}
 
@@ -169,7 +170,7 @@
     barrier = pltpu.get_barrier_semaphore()
     for other in member_order:
         pl.semaphore_signal(barrier, inc=1, device_id={"mem": other}, device_id_type=MESH)
-    for other in peer_order:
+    for other in peer_order + [partner]:
         pl.semaphore_signal(barrier, inc=1, device_id={"mp": other}, device_id_type=MESH)
 
     fetch("lengths", lengths_hbm, lengths)
@@ -188,35 +189,38 @@
                 device_id_type=MESH,
             ).start()
 
-    def send_peers(phase, source, target):
-        for other in peer_order:
-            pltpu.make_async_remote_copy(
-                src_ref=source,
-                dst_ref=target,
-                send_sem=send_sem.at[phase],
-                recv_sem=recv_sem.at[phase],
-                device_id={"mp": other},
-                device_id_type=MESH,
-            ).start()
-
     width = tokens.shape[1]
 
-    def sum_peers(phase, partial, staged, landed):
+    def send_peer(phase, source, target, other):
+        pltpu.make_async_remote_copy(
+            src_ref=source,
+            dst_ref=target,
+            send_sem=send_sem.at[phase],
+            recv_sem=recv_sem.at[phase],
+            device_id={"mp": other},
+            device_id_type=MESH,
+        ).start()
+
+    def sum_peers(phase, partial, staged, landed, summed, paired):
         unit_code = jnp.ceil(code_of(jnp.max(jnp.abs(partial), axis=1, keepdims=True)))
         steps = jnp.floor(partial * (STEPS / value_of(unit_code)) + 0.5)
         staged[:, :width] = steps.astype(jnp.int32).astype(jnp.int16)
         staged[:, width:] = (
             jnp.broadcast_to(unit_code, (rows, LANES)).astype(jnp.int32).astype(jnp.int16)
         )
-        send_peers(phase, staged, landed.at[mine])
-        landed[mine] = staged[...]
-        wait_bytes(landed.at[pl.ds(0, peers - 1)], recv_sem.at[phase])
+        for other in peer_order:
+            send_peer(phase, staged, landed.at[y], other)
+        landed[y] = staged[...]
+        wait_bytes(landed.at[pl.ds(0, ring - 1)], recv_sem.at[phase])
         total = jnp.zeros((rows, width), F32)
-        for j in range(peers):
+        for j in range(ring):
             part = landed[j].astype(jnp.int32).astype(F32)
             unit = value_of(part[:, width:]) * (1.0 / STEPS)
             total = total + part[:, :width] * jnp.concatenate([unit] * (width // LANES), axis=1)
-        return total
+        summed[...] = total
+        send_peer(phase + 1, summed, paired, partner)
+        wait_bytes(paired, recv_sem.at[phase + 1])
+        return total + paired[...]
 
     def wait_bytes(window, semaphore):
         pltpu.make_async_copy(window, window, semaphore).wait()
@@ -231,7 +235,7 @@
         s1[pl.ds(c, rows, stride=rows), :] = projected[:, c * LANES : (c + 1) * LANES]
     s1[pl.ds(HEADS + 2, rows, stride=rows), :] = jnp.broadcast_to(square_one, (rows, LANES))
 
-    pl.semaphore_wait(barrier, members - 1 + peers - 1)
+    pl.semaphore_wait(barrier, len(member_order) + len(peer_order) + 1)
 
     used = HEADS + 3
     send_members(
@@ -406,7 +410,7 @@
         [r5[pl.ds(h, rows, stride=HEADS), :].astype(BF16) for h in range(HEADS)], axis=1
     )
     partial = jnp.dot(attended, wout[...], preferred_element_type=F32)
-    after_f = (token_f + sum_peers(4, partial, s5b, r5b)).astype(BF16).astype(F32)
+    after_f = (token_f + sum_peers(4, partial, s5b, r5b, s5c, r5c)).astype(BF16).astype(F32)
     ready("gain_two", "wgate", "wup")
 
     scaled_mid = (after_f * gain_two[...].astype(F32)[None, :]).astype(BF16)
@@ -452,7 +456,7 @@
             pltpu.make_async_remote_copy(
                 src_ref=s6.at[k, other],
                 dst_ref=r6.at[me],
-                send_sem=send_sem.at[5],
+                send_sem=send_sem.at[6],
                 recv_sem=quarter_sem.at[k],
                 device_id={"mem": other * GROUPS + target},
                 device_id_type=MESH,
@@ -504,7 +508,7 @@
         pltpu.make_async_remote_copy(
             src_ref=s7,
             dst_ref=r7.at[me],
-            send_sem=send_sem.at[6],
+            send_sem=send_sem.at[7],
             recv_sem=group_sem.at[group],
             device_id={"mem": other},
             device_id_type=MESH,
@@ -531,15 +535,16 @@
             wdown[pl.ds(pl.multiple_of(source * span, LANES), span), :],
             preferred_element_type=F32,
         )
-    out_ref[...] = (after_f + sum_peers(7, down, s7b, r7b)).astype(BF16)
+    out_ref[...] = (after_f + sum_peers(8, down, s7b, r7b, s7c, r7c)).astype(BF16)
 
     wait_bytes(r1.at[pl.ds(0, members - 1), pl.ds(0, used)], send_sem.at[0])
     wait_bytes(r2.at[pl.ds(0, members - 1)], send_sem.at[1])
     wait_bytes(r4.at[pl.ds(0, (members - 1) * sent)], send_sem.at[2])
     wait_bytes(r5.at[pl.ds(0, (members - 1) * HEADS)], send_sem.at[3])
-    for phase, landed in ((4, r5b), (7, r7b)):
-        wait_bytes(landed.at[pl.ds(0, peers - 1)], send_sem.at[phase])
-    for phase, landed in ((5, r6), (6, r7)):
+    for phase, landed, paired in ((4, r5b, r5c), (8, r7b, r7c)):
+        wait_bytes(landed.at[pl.ds(0, ring - 1)], send_sem.at[phase])
+        wait_bytes(paired, send_sem.at[phase + 1])
+    for phase, landed in ((6, r6), (7, r7)):
         wait_bytes(landed.at[pl.ds(0, members - 1)], send_sem.at[phase])
 
 
@@ -598,7 +603,9 @@
         pltpu.VMEM((HEADS, LANES), F32),
         pltpu.VMEM((members * HEADS, LANES), F32),
         pltpu.VMEM((rows, width_part + LANES), jnp.int16),
-        pltpu.VMEM((peers, rows, width_part + LANES), jnp.int16),
+        pltpu.VMEM((peers // 2, rows, width_part + LANES), jnp.int16),
+        pltpu.VMEM((rows, width_part), F32),
+        pltpu.VMEM((rows, width_part), F32),
         pltpu.VMEM((2 * GROUPS * rows * LINES, LANES), F32),
         pltpu.VMEM((GROUPS, GROUPS, 2 * short, LANES), jnp.int16),
         pltpu.VMEM((members, 2 * short, LANES), jnp.int16),
@@ -606,11 +613,13 @@
         pltpu.VMEM((members, short, LANES), BF16),
         pltpu.VMEM((GROUPS * rows * LINES, LANES), F32),
         pltpu.VMEM((rows, width_part + LANES), jnp.int16),
-        pltpu.VMEM((peers, rows, width_part + LANES), jnp.int16),
+        pltpu.VMEM((peers // 2, rows, width_part + LANES), jnp.int16),
+        pltpu.VMEM((rows, width_part), F32),
+        pltpu.VMEM((rows, width_part), F32),
         pltpu.SemaphoreType.DMA,
         pltpu.SemaphoreType.DMA((6 + 6 * PIECES + 2,)),
-        pltpu.SemaphoreType.DMA((8,)),
-        pltpu.SemaphoreType.DMA((8,)),
+        pltpu.SemaphoreType.DMA((10,)),
+        pltpu.SemaphoreType.DMA((10,)),
         pltpu.SemaphoreType.DMA((GROUPS,)),
         pltpu.SemaphoreType.DMA((GROUPS,)),
     ]

time: 55 us -> 56.3 us (1.024)
  Pallas kernels: 53.4 us -> 54.7 us
    pallas_call x1, Pallas kernels: 53.4 us -> 54.7 us  [local(): pl.pallas_call(functools.partial(kernel, members, peers, width_part * mem...]
where the time goes in v6:
time: 56.3 us; the launch traced here: 56 us
  Pallas kernels  54.7 us (97%)
  local copies, waits for them, and re-layouts  1.32 us (2%)
    pallas_call x1, Pallas kernels, local(): pl.pallas_call(functools.partial(kernel, members, peers, width_part * mem...  54.7 us
    unnamed x1, local copies, waits for them, and re-layouts  1.32 us

profile of v6, /device:TPU:1, one launch (start us, length us, event | category | flops | bytes accessed | tf_op | source)
XLA Modules:
  0.0 56.0 jit_solution(11013385137901027889)
XLA Ops:
  0.0 54.7 %decoder_layer.1 = bf16[16,512]{1,0:T(8,128)(2,1)} custom-call(s32[4]{0:T(128)} %lengths_hbm.1, bf16[16,512]{1,0:T(8,128)(2,1)} %tokens_hbm.1, bf16[512]{0:T(512)(128)(2,1)} %gain_one_hbm.1, bf16[512]{0:T(512)(128)(2,1)} %gain_two_hbm.1, f32[1,128]{1,0:T(1,128)} %constant.2.clone.freq_hbm, s32[4,512]{1,0:T(4,128)} %table_hbm.1, bf16[512,1280]{1,0:T(8,128)(2,1)} %wqkv_hbm.1, ...), custom_call_target="tpu_custom_call" | custom-call | tf_op jit(solution)/shard_map/decoder_layer/pallas_call | solution.py:626
  54.7 1.3 %copy.15 = bf16[16,512]{1,0:T(8,128)(2,1)} copy(bf16[16,512]{1,0:T(8,128)(2,1)} %decoder_layer.1) | data formatting | bytes 32768

commit v7 on v5

--- a/solution.py
+++ b/solution.py
@@ -22,7 +22,8 @@
 REQUESTS = 4
 GROUP = NEW * HEADS
 OWNER = 256
-TILE = 32
+RUN = 4
+TILE = 9
 PARTIAL = 16
 GROUPS = 4
 LINES = 8
@@ -276,12 +277,30 @@
         held = jnp.where(held > 0, held + r * OWNER, 0)
         code = code + jnp.where(table[r : r + 1, :] == slot_ids, held, 0)
     code = jnp.sum(code, axis=1, keepdims=True)
-    diagonal = lax.broadcasted_iota(jnp.int32, (slots, slots), 0) == lax.broadcasted_iota(
-        jnp.int32, (slots, slots), 1
-    )
-    code = jnp.sum(jnp.where(diagonal, code, 0), axis=0, keepdims=True)
-    owner_row = code // OWNER
-    codes[0:1, :] = code
+    sub = lax.broadcasted_iota(jnp.int32, (slots, slots), 0)
+    lane = lax.broadcasted_iota(jnp.int32, (slots, slots), 1)
+    code_line = jnp.sum(jnp.where(sub == lane, code, 0), axis=0, keepdims=True)
+    owner_column = jnp.where(code > 0, code >> 8, REQUESTS)
+    owner_line = jnp.where(code_line > 0, code_line >> 8, REQUESTS)
+    ahead = jnp.where((owner_line == owner_column) & (lane < sub), 1, 0)
+    place_column = jnp.sum(ahead, axis=1, keepdims=True)
+    positions = codes.shape[1]
+    run_ids = lax.broadcasted_iota(jnp.int32, (1, positions), 1) * RUN
+    run_owner = jnp.zeros((1, positions), jnp.int32)
+    start = jnp.zeros((1, 1), jnp.int32)
+    for r in range(REQUESTS):
+        if r > 0:
+            run_owner = run_owner + jnp.where(run_ids >= start, 1, 0)
+        place_column = place_column + jnp.where(owner_column == r, start, 0)
+        number = jnp.sum(jnp.where(owner_line == r, 1, 0), axis=1, keepdims=True)
+        start = start + ((number + (RUN - 1)) & -RUN)
+    place_column = jnp.where(code > 0, place_column, -1)
+    position_ids = lax.broadcasted_iota(jnp.int32, (slots, positions), 1)
+    entry = lax.broadcasted_iota(jnp.int32, (slots, positions), 0) * OWNER + (code & (OWNER - 1))
+    entry = jnp.where(position_ids == place_column, entry, 0)
+    codes[0:1, :] = jnp.sum(entry, axis=0, keepdims=True)
+    codes[1:2, :] = run_owner
+    owner_row = run_owner[:, :LANES]
     to_scalars = pltpu.make_async_copy(codes, slot_codes, code_sem)
     to_scalars.start()
 
@@ -296,30 +315,35 @@
     to_scalars.wait()
     ready("keys")
 
-    def slot_of(slot):
-        value = slot_codes[0, slot]
-        return value // OWNER, lax.rem(value, OWNER)
+    def run_of(run):
+        entries = [slot_codes[0, run * RUN + i] for i in range(RUN)]
+        return slot_codes[1, run], [(e >> 8, e & (OWNER - 1)) for e in entries]
 
     def score_step(step, best):
         for j in range(TILE):
-            slot = step * TILE + j
-            owner, count = slot_of(slot)
+            run = step * TILE + j
+            owner, members_of = run_of(run)
             score = lax.dot_general(
                 queries[owner],
-                keys[slot],
+                jnp.concatenate([keys[slot] for slot, _ in members_of], axis=0),
                 (((1,), (1,)), ((), ())),
                 preferred_element_type=F32,
             )
-            score = jnp.where(lane_group < count, score, FLOOR_SCORE)
-            scores[slot] = score
-            best = jnp.where(lane_group == slot, jnp.max(score, axis=1, keepdims=True), best)
+            tops = []
+            for i, (_, count) in enumerate(members_of):
+                part = slice(i * LANES, (i + 1) * LANES)
+                tops.append(jnp.where(lane_group < count, score[:, part], FLOOR_SCORE))
+                scores[run, :, part] = tops[-1]
+            top = jnp.max(functools.reduce(jnp.maximum, tops), axis=1, keepdims=True)
+            best = jnp.where(lane_group == run, top, best)
         return best
 
     floor = jnp.full((GROUP, LANES), FLOOR_SCORE, F32)
-    slot_best = lax.fori_loop(0, slots // TILE, score_step, floor)
+    runs = scores.shape[0]
+    run_best = lax.fori_loop(0, runs // TILE, score_step, floor)
     best = []
     for r in range(REQUESTS):
-        own = jnp.where(owner_row == r, slot_best, FLOOR_SCORE)
+        own = jnp.where(owner_row == r, run_best, FLOOR_SCORE)
         best.append(jnp.broadcast_to(jnp.max(own, axis=1, keepdims=True), (GROUP, LANES)))
         tops_ref[r] = best[r]
     ready("values")
@@ -327,14 +351,23 @@
     def value_step(step, carry):
         sums, mixed = carry[0], list(carry[1])
         for j in range(TILE):
-            slot = step * TILE + j
-            owner, _ = slot_of(slot)
-            weight = jnp.exp2((scores[slot] - tops_ref[owner]) * factor)
-            sums = jnp.where(lane_group == slot, jnp.sum(weight, axis=1, keepdims=True), sums)
-            high = weight.astype(BF16)
-            low = (weight - high.astype(F32)).astype(BF16)
+            run = step * TILE + j
+            owner, members_of = run_of(run)
+            top = tops_ref[owner]
+            weights, highs, lows = [], [], []
+            for i in range(RUN):
+                weight = jnp.exp2((scores[run, :, i * LANES : (i + 1) * LANES] - top) * factor)
+                weights.append(weight)
+                highs.append(weight.astype(BF16))
+                lows.append((weight - highs[-1].astype(F32)).astype(BF16))
+            total = jnp.sum(functools.reduce(jnp.add, weights), axis=1, keepdims=True)
+            sums = jnp.where(lane_group == run, total, sums)
             both = jnp.dot(
-                jnp.concatenate([high, low], axis=0), values[slot], preferred_element_type=F32
+                jnp.concatenate(
+                    [jnp.concatenate(highs, axis=1), jnp.concatenate(lows, axis=1)], axis=0
+                ),
+                jnp.concatenate([values[slot] for slot, _ in members_of], axis=0),
+                preferred_element_type=F32,
             )
             both = both[:GROUP] + both[GROUP:]
             for r in range(REQUESTS):
@@ -342,7 +375,7 @@
         return sums, tuple(mixed)
 
     zero = jnp.zeros((GROUP, LANES), F32)
-    slot_sums, mixed = lax.fori_loop(0, slots // TILE, value_step, (zero, (zero,) * REQUESTS))
+    run_sums, mixed = lax.fori_loop(0, runs // TILE, value_step, (zero, (zero,) * REQUESTS))
     lane_head = lax.broadcasted_iota(jnp.int32, (HEADS, LANES), 1) // (LANES // HEADS)
     by_head = lane_head == lax.broadcasted_iota(jnp.int32, (HEADS, LANES), 0)
 
@@ -354,7 +387,7 @@
         return jnp.broadcast_to(column, (HEADS, LANES))
 
     for r in range(REQUESTS):
-        own = jnp.where(owner_row == r, slot_sums, 0.0)
+        own = jnp.where(owner_row == r, run_sums, 0.0)
         whole = jnp.broadcast_to(jnp.sum(own, axis=1, keepdims=True), (GROUP, LANES))
         for t in range(NEW):
             part = slice(t * HEADS, (t + 1) * HEADS)
@@ -562,6 +595,7 @@
     rows, width_part = tokens.shape
     slots, _, block_len, head_dim = paged_key_store.shape
     short = rows * LINES // GROUPS
+    runs = slots // RUN + REQUESTS
     exponents = np.arange(head_dim // 2, dtype=np.float32) * np.float32(
         -2.0 * math.log(ROPE_BASE) / head_dim
     )
@@ -585,10 +619,10 @@
         pltpu.VMEM(up_weight.shape, BF16),
         pltpu.VMEM(down_weight.shape, BF16),
         pltpu.VMEM((REQUESTS, GROUP, head_dim), BF16),
-        pltpu.VMEM((8, slots), jnp.int32),
-        pltpu.SMEM((8, slots), jnp.int32),
+        pltpu.VMEM((8, 2 * LANES), jnp.int32),
+        pltpu.SMEM((8, 2 * LANES), jnp.int32),
         pltpu.VMEM((REQUESTS, GROUP, LANES), F32),
-        pltpu.VMEM((slots, GROUP, LANES), F32),
+        pltpu.VMEM((runs, GROUP, RUN * LANES), F32),
         pltpu.VMEM((rows * rows, LANES), F32),
         pltpu.VMEM((members, rows, LANES), F32),
         pltpu.VMEM((16, LANES), BF16),

time: 55 us -> 54.2 us (0.985)
  Pallas kernels: 53.4 us -> 52.6 us
    pallas_call x1, Pallas kernels: 53.4 us -> 52.6 us  [local(): pl.pallas_call(functools.partial(kernel, members, peers, width_part * mem...]
where the time goes in v7:
time: 54.2 us; the launch traced here: 53.9 us
  Pallas kernels  52.6 us (97%)
  local copies, waits for them, and re-layouts  1.32 us (2%)
    pallas_call x1, Pallas kernels, local(): pl.pallas_call(functools.partial(kernel, members, peers, width_part * mem...  52.6 us
    unnamed x1, local copies, waits for them, and re-layouts  1.32 us

profile of v7, /device:TPU:1, one launch (start us, length us, event | category | flops | bytes accessed | tf_op | source)
XLA Modules:
  0.0 53.9 jit_solution(13833421259761054966)
XLA Ops:
  0.0 52.6 %decoder_layer.1 = bf16[16,512]{1,0:T(8,128)(2,1)} custom-call(s32[4]{0:T(128)} %lengths_hbm.1, bf16[16,512]{1,0:T(8,128)(2,1)} %tokens_hbm.1, bf16[512]{0:T(512)(128)(2,1)} %gain_one_hbm.1, bf16[512]{0:T(512)(128)(2,1)} %gain_two_hbm.1, f32[1,128]{1,0:T(1,128)} %constant.2.clone.freq_hbm, s32[4,512]{1,0:T(4,128)} %table_hbm.1, bf16[512,1280]{1,0:T(8,128)(2,1)} %wqkv_hbm.1, ...), custom_call_target="tpu_custom_call" | custom-call | tf_op jit(solution)/shard_map/decoder_layer/pallas_call | solution.py:651
  52.6 1.3 %copy.15 = bf16[16,512]{1,0:T(8,128)(2,1)} copy(bf16[16,512]{1,0:T(8,128)(2,1)} %decoder_layer.1) | data formatting | bytes 32768

commit v8 on v7

--- a/solution.py
+++ b/solution.py
@@ -23,7 +23,7 @@
 GROUP = NEW * HEADS
 OWNER = 256
 RUN = 4
-TILE = 9
+TILE = 18
 PARTIAL = 16
 GROUPS = 4
 LINES = 8
@@ -165,7 +165,9 @@
 
     fetch("tokens", tokens_hbm, tokens)
     fetch("gain_one", gain_one_hbm, gain_one)
-    fetch("wqkv", wqkv_hbm, wqkv, PIECES)
+    fetch("wqkv", wqkv_hbm, wqkv, 2 * PIECES)
+    fetch("lengths", lengths_hbm, lengths)
+    fetch("freq", freq_hbm, freq)
 
     barrier = pltpu.get_barrier_semaphore()
     for other in member_order:
@@ -173,8 +175,6 @@
     for other in peer_order:
         pl.semaphore_signal(barrier, inc=1, device_id={"mp": other}, device_id_type=MESH)
 
-    fetch("lengths", lengths_hbm, lengths)
-    fetch("freq", freq_hbm, freq)
     fetch("table", table_hbm, table)
     fetch("gain_two", gain_two_hbm, gain_two)
 
@@ -226,29 +226,28 @@
     token_f = tokens[...].astype(F32)
     scaled_in = (token_f * gain_one[...].astype(F32)[None, :]).astype(BF16)
     square_one = jnp.sum(token_f * token_f, axis=1, keepdims=True)
-    ready("wqkv")
-    projected = jnp.dot(scaled_in, wqkv[...], preferred_element_type=F32)
-    for c in range(HEADS + 2):
-        s1[pl.ds(c, rows, stride=rows), :] = projected[:, c * LANES : (c + 1) * LANES]
-    s1[pl.ds(HEADS + 2, rows, stride=rows), :] = jnp.broadcast_to(square_one, (rows, LANES))
-
-    pl.semaphore_wait(barrier, members - 1 + peers - 1)
-
-    used = HEADS + 3
-    send_members(
-        0, lambda other: s1.at[pl.ds(other * rows, used)], r1.at[me, pl.ds(0, used)]
-    )
-    r1[me] = s1[pl.ds(pl.multiple_of(me * rows, rows), rows), :]
-
-    fetch("keys", keys_hbm.at[:, 0], keys, PIECES)
-    fetch("values", values_hbm.at[:, 0], values, PIECES)
-
     request, place = me // NEW, lax.rem(me, NEW)
     ready("lengths", "freq")
     position = (lengths[request] + place).astype(F32)
     sine, cosine = sine_cosine(position * freq[...])
     lane_row = lax.broadcasted_iota(jnp.int32, (1, LANES), 1)
     sine = jnp.where(lane_row < LANES // 2, -sine, sine)
+    ready("wqkv")
+    projected = jnp.dot(scaled_in, wqkv[...], preferred_element_type=F32)
+    for c in range(HEADS + 2):
+        s1[pl.ds(c, rows, stride=rows), :] = projected[:, c * LANES : (c + 1) * LANES]
+    s1[pl.ds(HEADS + 2, rows, stride=rows), :] = jnp.broadcast_to(square_one, (rows, LANES))
+
+    pl.semaphore_wait(barrier, members - 1 + peers - 1)
+
+    used = HEADS + 3
+    send_members(
+        0, lambda other: s1.at[pl.ds(other * rows, used)], r1.at[me, pl.ds(0, used)]
+    )
+    r1[me] = s1[pl.ds(pl.multiple_of(me * rows, rows), rows), :]
+
+    fetch("keys", keys_hbm.at[:, 0], keys, PIECES)
+    fetch("values", values_hbm.at[:, 0], values, PIECES)
 
     wait_bytes(r1.at[pl.ds(0, members - 1), pl.ds(0, used)], recv_sem.at[0])
     total = r1[0]
@@ -259,8 +258,8 @@
     turned = total * cosine + pltpu.roll(total, LANES // 2, 1) * sine
     head_row = lax.broadcasted_iota(jnp.int32, total.shape, 0)
     s2[...] = jnp.where(head_row <= HEADS, turned, total).astype(BF16)
+    send_members(1, lambda other: s2, r2.at[me])
     r2[me] = s2[...]
-    send_members(1, lambda other: s2, r2.at[me])
     fetch("wout", wout_hbm, wout, 2)
     fetch("wgate", wgate_hbm, wgate, PIECES)
     fetch("wup", wup_hbm, wup, PIECES)
@@ -430,8 +429,8 @@
         mix = mix + r4[j * PARTIAL : j * PARTIAL + HEADS, :] * to_column(shrink[j : j + 1])
     s5[...] = mix / whole
     own_rows = pl.ds(pl.multiple_of(me * HEADS, HEADS), HEADS)
+    send_members(3, lambda other: s5, r5.at[own_rows])
     r5[own_rows, :] = s5[...]
-    send_members(3, lambda other: s5, r5.at[own_rows])
     ready("wout")
     wait_bytes(r5.at[pl.ds(0, (members - 1) * HEADS)], recv_sem.at[3])
 
@@ -532,7 +531,6 @@
         gate = gates[r] * inverse_two[r : r + 1]
         hidden.append(gate / (1.0 + jnp.exp(-gate)) * (ups[r] * inverse_two[r : r + 1]))
     s7[...] = jnp.concatenate(hidden, axis=0).astype(BF16)
-    r7[me] = s7[...]
     for other in member_order:
         pltpu.make_async_remote_copy(
             src_ref=s7,
@@ -542,6 +540,7 @@
             device_id={"mem": other},
             device_id_type=MESH,
         ).start()
+    r7[me] = s7[...]
     ready("wdown")
 
     down = jnp.zeros((rows, wdown.shape[1]), F32)
@@ -642,7 +641,7 @@
         pltpu.VMEM((rows, width_part + LANES), jnp.int16),
         pltpu.VMEM((peers, rows, width_part + LANES), jnp.int16),
         pltpu.SemaphoreType.DMA,
-        pltpu.SemaphoreType.DMA((6 + 6 * PIECES + 2,)),
+        pltpu.SemaphoreType.DMA((6 + 7 * PIECES + 2,)),
         pltpu.SemaphoreType.DMA((8,)),
         pltpu.SemaphoreType.DMA((8,)),
         pltpu.SemaphoreType.DMA((GROUPS,)),
@@ -650,7 +649,7 @@
     ]
     return pl.pallas_call(
         functools.partial(kernel, members, peers, width_part * members),
-        out_shape=jax.ShapeDtypeStruct(tokens.shape, BF16),
+        out_shape=pltpu.VMEM(tokens.shape, BF16),
         in_specs=[any_spec] * 13,
         out_specs=vmem_spec,
         scratch_shapes=scratch,

time: 54.2 us -> 52.2 us (0.963)
  Pallas kernels: 52.6 us -> 51.4 us
  local copies, waits for them, and re-layouts: 1.32 us -> 0.61 us
    pallas_call x1, Pallas kernels: 52.6 us -> 51.4 us  [local(): pl.pallas_call(functools.partial(kernel, members, peers, width_part * mem...]
    unnamed x1, local copies, waits for them, and re-layouts: 1.32 us -> 0.61 us
where the time goes in v8:
time: 52.2 us; the launch traced here: 52.1 us
  Pallas kernels  51.4 us (98%)
  local copies, waits for them, and re-layouts  0.61 us (1%)
    pallas_call x1, Pallas kernels, local(): pl.pallas_call(functools.partial(kernel, members, peers, width_part * mem...  51.4 us

profile of v8, /device:TPU:1, one launch (start us, length us, event | category | flops | bytes accessed | tf_op | source)
XLA Modules:
  0.0 52.1 jit_solution(15336879763873786956)
XLA Ops:
  0.0 51.4 %decoder_layer.1 = bf16[16,512]{1,0:T(8,128)(2,1)S(1)} custom-call(s32[4]{0:T(128)} %lengths_hbm.1, bf16[16,512]{1,0:T(8,128)(2,1)} %tokens_hbm.1, bf16[512]{0:T(512)(128)(2,1)} %gain_one_hbm.1, bf16[512]{0:T(512)(128)(2,1)} %gain_two_hbm.1, f32[1,128]{1,0:T(1,128)} %constant.2.clone.freq_hbm, s32[4,512]{1,0:T(4,128)} %table_hbm.1, ...), custom_call_target="tpu_custom_call" | custom-call | tf_op jit(solution)/shard_map/decoder_layer/pallas_call | solution.py:650
  51.4 0.6 %copy.15 = bf16[16,512]{1,0:T(8,128)(2,1)} copy(bf16[16,512]{1,0:T(8,128)(2,1)S(1)} %decoder_layer.1) | data formatting | bytes 32768

commit v9 on v8

--- a/solution.py
+++ b/solution.py
@@ -318,23 +318,38 @@
         entries = [slot_codes[0, run * RUN + i] for i in range(RUN)]
         return slot_codes[1, run], [(e >> 8, e & (OWNER - 1)) for e in entries]
 
+    blank = jnp.zeros((GROUP, LANES), BF16)
+
     def score_step(step, best):
-        for j in range(TILE):
-            run = step * TILE + j
-            owner, members_of = run_of(run)
-            score = lax.dot_general(
-                queries[owner],
-                jnp.concatenate([keys[slot] for slot, _ in members_of], axis=0),
-                (((1,), (1,)), ((), ())),
-                preferred_element_type=F32,
+        for j in range(0, TILE, 2):
+            pair = [(step * TILE + j + i,) + run_of(step * TILE + j + i) for i in range(2)]
+            first, second = (queries[owner] for _, owner, _ in pair)
+            left = jnp.concatenate(
+                [
+                    jnp.concatenate([first, blank], axis=1),
+                    jnp.concatenate([blank, second], axis=1),
+                ],
+                axis=0,
             )
-            tops = []
-            for i, (_, count) in enumerate(members_of):
-                part = slice(i * LANES, (i + 1) * LANES)
-                tops.append(jnp.where(lane_group < count, score[:, part], FLOOR_SCORE))
-                scores[run, :, part] = tops[-1]
-            top = jnp.max(functools.reduce(jnp.maximum, tops), axis=1, keepdims=True)
-            best = jnp.where(lane_group == run, top, best)
+            right = jnp.concatenate(
+                [
+                    jnp.concatenate([keys[slot] for slot, _ in members_of], axis=0)
+                    for _, _, members_of in pair
+                ],
+                axis=1,
+            )
+            both = lax.dot_general(
+                left, right, (((1,), (1,)), ((), ())), preferred_element_type=F32
+            )
+            for half, (run, _, members_of) in enumerate(pair):
+                score = both[half * GROUP : (half + 1) * GROUP]
+                tops = []
+                for i, (_, count) in enumerate(members_of):
+                    part = slice(i * LANES, (i + 1) * LANES)
+                    tops.append(jnp.where(lane_group < count, score[:, part], FLOOR_SCORE))
+                    scores[run, :, part] = tops[-1]
+                top = jnp.max(functools.reduce(jnp.maximum, tops), axis=1, keepdims=True)
+                best = jnp.where(lane_group == run, top, best)
         return best
 
     floor = jnp.full((GROUP, LANES), FLOOR_SCORE, F32)
@@ -457,10 +472,9 @@
 
     def multiply(k):
         columns = pl.ds(pl.multiple_of(lax.rem(group + k, GROUPS) * span, LANES), span)
-        return [
-            jnp.dot(scaled_mid, weight[:, columns], preferred_element_type=F32)
-            for weight in (wgate, wup)
-        ]
+        both = jnp.concatenate([wgate[:, columns], wup[:, columns]], axis=1)
+        both = jnp.dot(scaled_mid, both, preferred_element_type=F32)
+        return both[:, :span], both[:, span:]
 
     def ship(k, parts):
         target = lax.rem(group + k, GROUPS)

time: 52.2 us -> 52.1 us (level)
  no operation moved by 1% of the time
where the time goes in v9:
time: 52.1 us; the launch traced here: 51.9 us
  Pallas kernels  51.3 us (98%)
  local copies, waits for them, and re-layouts  0.61 us (1%)
    pallas_call x1, Pallas kernels, local(): pl.pallas_call(functools.partial(kernel, members, peers, width_part * mem...  51.3 us

profile of v9, /device:TPU:1, one launch (start us, length us, event | category | flops | bytes accessed | tf_op | source)
XLA Modules:
  0.0 51.9 jit_solution(10182362746282518691)
XLA Ops:
  0.0 51.3 %decoder_layer.1 = bf16[16,512]{1,0:T(8,128)(2,1)S(1)} custom-call(s32[4]{0:T(128)} %lengths_hbm.1, bf16[16,512]{1,0:T(8,128)(2,1)} %tokens_hbm.1, bf16[512]{0:T(512)(128)(2,1)} %gain_one_hbm.1, bf16[512]{0:T(512)(128)(2,1)} %gain_two_hbm.1, f32[1,128]{1,0:T(1,128)} %constant.2.clone.freq_hbm, s32[4,512]{1,0:T(4,128)} %table_hbm.1, ...), custom_call_target="tpu_custom_call" | custom-call | tf_op jit(solution)/shard_map/decoder_layer/pallas_call | solution.py:664
  51.3 0.6 %copy.15 = bf16[16,512]{1,0:T(8,128)(2,1)} copy(bf16[16,512]{1,0:T(8,128)(2,1)S(1)} %decoder_layer.1) | data formatting | bytes 32768

commit v10 on v9

--- a/solution.py
+++ b/solution.py
@@ -247,7 +247,6 @@
     r1[me] = s1[pl.ds(pl.multiple_of(me * rows, rows), rows), :]
 
     fetch("keys", keys_hbm.at[:, 0], keys, PIECES)
-    fetch("values", values_hbm.at[:, 0], values, PIECES)
 
     wait_bytes(r1.at[pl.ds(0, members - 1), pl.ds(0, used)], recv_sem.at[0])
     total = r1[0]
@@ -260,10 +259,10 @@
     s2[...] = jnp.where(head_row <= HEADS, turned, total).astype(BF16)
     send_members(1, lambda other: s2, r2.at[me])
     r2[me] = s2[...]
+    fetch("values", values_hbm.at[:, 0], values, PIECES)
     fetch("wout", wout_hbm, wout, 2)
     fetch("wgate", wgate_hbm, wgate, PIECES)
     fetch("wup", wup_hbm, wup, PIECES)
-    fetch("wdown", wdown_hbm, wdown, PIECES)
 
     ready("table")
     first_slot = me * slots
@@ -417,6 +416,7 @@
         r4.at[pl.ds(me * PARTIAL, sent)],
     )
     r4[mine_4, :] = s4[mine_4, :]
+    fetch("wdown", wdown_hbm, wdown, PIECES)
 
     row_queries = r2[me].astype(F32)[:HEADS]
     own_scores, own_values = [], []

time: 52.1 us -> 52.1 us (level)
  no operation moved by 1% of the time
where the time goes in v10:
time: 52.1 us; the launch traced here: 51.9 us
  Pallas kernels  51.3 us (98%)
  local copies, waits for them, and re-layouts  0.61 us (1%)
    pallas_call x1, Pallas kernels, local(): pl.pallas_call(functools.partial(kernel, members, peers, width_part * mem...  51.3 us

profile of v10, /device:TPU:1, one launch (start us, length us, event | category | flops | bytes accessed | tf_op | source)
XLA Modules:
  0.0 51.9 jit_solution(7474636703091162928)
XLA Ops:
  0.0 51.3 %decoder_layer.1 = bf16[16,512]{1,0:T(8,128)(2,1)S(1)} custom-call(s32[4]{0:T(128)} %lengths_hbm.1, bf16[16,512]{1,0:T(8,128)(2,1)} %tokens_hbm.1, bf16[512]{0:T(512)(128)(2,1)} %gain_one_hbm.1, bf16[512]{0:T(512)(128)(2,1)} %gain_two_hbm.1, f32[1,128]{1,0:T(1,128)} %constant.2.clone.freq_hbm, s32[4,512]{1,0:T(4,128)} %table_hbm.1, ...), custom_call_target="tpu_custom_call" | custom-call | tf_op jit(solution)/shard_map/decoder_layer/pallas_call | solution.py:664
  51.3 0.6 %copy.15 = bf16[16,512]{1,0:T(8,128)(2,1)} copy(bf16[16,512]{1,0:T(8,128)(2,1)S(1)} %decoder_layer.1) | data formatting | bytes 32768

commit v11 on v10

--- a/solution.py
+++ b/solution.py
@@ -23,7 +23,7 @@
 GROUP = NEW * HEADS
 OWNER = 256
 RUN = 4
-TILE = 18
+TILE = 36
 PARTIAL = 16
 GROUPS = 4
 LINES = 8

time: 52.1 us -> 51.7 us (level)
  no operation moved by 1% of the time
where the time goes in v11:
time: 51.7 us; the launch traced here: 51.5 us
  Pallas kernels  50.9 us (98%)
  local copies, waits for them, and re-layouts  0.61 us (1%)
    pallas_call x1, Pallas kernels, local(): pl.pallas_call(functools.partial(kernel, members, peers, width_part * mem...  50.9 us

profile of v11, /device:TPU:1, one launch (start us, length us, event | category | flops | bytes accessed | tf_op | source)
XLA Modules:
  0.0 51.5 jit_solution(838383218921021923)
XLA Ops:
  0.0 50.9 %decoder_layer.1 = bf16[16,512]{1,0:T(8,128)(2,1)S(1)} custom-call(s32[4]{0:T(128)} %lengths_hbm.1, bf16[16,512]{1,0:T(8,128)(2,1)} %tokens_hbm.1, bf16[512]{0:T(512)(128)(2,1)} %gain_one_hbm.1, bf16[512]{0:T(512)(128)(2,1)} %gain_two_hbm.1, f32[1,128]{1,0:T(1,128)} %constant.2.clone.freq_hbm, s32[4,512]{1,0:T(4,128)} %table_hbm.1, ...), custom_call_target="tpu_custom_call" | custom-call | tf_op jit(solution)/shard_map/decoder_layer/pallas_call | solution.py:664
  50.9 0.6 %copy.15 = bf16[16,512]{1,0:T(8,128)(2,1)} copy(bf16[16,512]{1,0:T(8,128)(2,1)S(1)} %decoder_layer.1) | data formatting | bytes 32768

commit v12 on v11

--- a/solution.py
+++ b/solution.py
@@ -248,6 +248,17 @@
 
     fetch("keys", keys_hbm.at[:, 0], keys, PIECES)
 
+    ready("table")
+    first_slot = me * slots
+    max_blocks = table.shape[1]
+    block_start = lax.broadcasted_iota(jnp.int32, (1, max_blocks), 1) * block_len
+    slot_ids = first_slot + lax.broadcasted_iota(jnp.int32, (slots, max_blocks), 0)
+    code = jnp.zeros((slots, max_blocks), jnp.int32)
+    for r in range(REQUESTS):
+        held = jnp.clip(lengths[r] - block_start, 0, block_len)
+        held = jnp.where(held > 0, held + r * OWNER, 0)
+        code = code + jnp.where(table[r : r + 1, :] == slot_ids, held, 0)
+    code = jnp.sum(code, axis=1, keepdims=True)
     wait_bytes(r1.at[pl.ds(0, members - 1), pl.ds(0, used)], recv_sem.at[0])
     total = r1[0]
     for j in range(1, members):
@@ -260,21 +271,7 @@
     send_members(1, lambda other: s2, r2.at[me])
     r2[me] = s2[...]
     fetch("values", values_hbm.at[:, 0], values, PIECES)
-    fetch("wout", wout_hbm, wout, 2)
-    fetch("wgate", wgate_hbm, wgate, PIECES)
-    fetch("wup", wup_hbm, wup, PIECES)
-
-    ready("table")
-    first_slot = me * slots
-    max_blocks = table.shape[1]
-    block_start = lax.broadcasted_iota(jnp.int32, (1, max_blocks), 1) * block_len
-    slot_ids = first_slot + lax.broadcasted_iota(jnp.int32, (slots, max_blocks), 0)
-    code = jnp.zeros((slots, max_blocks), jnp.int32)
-    for r in range(REQUESTS):
-        held = jnp.clip(lengths[r] - block_start, 0, block_len)
-        held = jnp.where(held > 0, held + r * OWNER, 0)
-        code = code + jnp.where(table[r : r + 1, :] == slot_ids, held, 0)
-    code = jnp.sum(code, axis=1, keepdims=True)
+
     sub = lax.broadcasted_iota(jnp.int32, (slots, slots), 0)
     lane = lax.broadcasted_iota(jnp.int32, (slots, slots), 1)
     code_line = jnp.sum(jnp.where(sub == lane, code, 0), axis=0, keepdims=True)
@@ -301,6 +298,9 @@
     owner_row = run_owner[:, :LANES]
     to_scalars = pltpu.make_async_copy(codes, slot_codes, code_sem)
     to_scalars.start()
+    fetch("wout", wout_hbm, wout, 2)
+    fetch("wgate", wgate_hbm, wgate, PIECES)
+    fetch("wup", wup_hbm, wup, PIECES)
 
     wait_bytes(r2.at[pl.ds(0, members - 1)], recv_sem.at[1])
 

time: 51.7 us -> 51.7 us (level)
  no operation moved by 1% of the time
where the time goes in v12:
time: 51.7 us; the launch traced here: 51.5 us
  Pallas kernels  50.9 us (98%)
  local copies, waits for them, and re-layouts  0.61 us (1%)
    pallas_call x1, Pallas kernels, local(): pl.pallas_call(functools.partial(kernel, members, peers, width_part * mem...  50.9 us

profile of v12, /device:TPU:1, one launch (start us, length us, event | category | flops | bytes accessed | tf_op | source)
XLA Modules:
  0.0 51.5 jit_solution(4773993418338059839)
XLA Ops:
  0.0 50.9 %decoder_layer.1 = bf16[16,512]{1,0:T(8,128)(2,1)S(1)} custom-call(s32[4]{0:T(128)} %lengths_hbm.1, bf16[16,512]{1,0:T(8,128)(2,1)} %tokens_hbm.1, bf16[512]{0:T(512)(128)(2,1)} %gain_one_hbm.1, bf16[512]{0:T(512)(128)(2,1)} %gain_two_hbm.1, f32[1,128]{1,0:T(1,128)} %constant.2.clone.freq_hbm, s32[4,512]{1,0:T(4,128)} %table_hbm.1, ...), custom_call_target="tpu_custom_call" | custom-call | tf_op jit(solution)/shard_map/decoder_layer/pallas_call | solution.py:664
  50.9 0.6 %copy.15 = bf16[16,512]{1,0:T(8,128)(2,1)} copy(bf16[16,512]{1,0:T(8,128)(2,1)S(1)} %decoder_layer.1) | data formatting | bytes 32768
